TPU v7x, 32 devices: a whole 2x2x4 slice. The times are simulated.
32 devices in a mesh: seq: 8 (over z, x), grp: 4 (over y, core).
Axes of the slice: x: 2, y: 2, z: 4, core: 2. Of those that a mesh axis runs over, the one named last changes fastest.
Arguments:
- query_vecs: bfloat16 [16384, 1024], P(('seq', 'grp')), may hold values from -6 to 6
- key_vecs: bfloat16 [16384, 1024], P(('seq', 'grp')), may hold values from -6 to 6
- value_vecs: bfloat16 [16384, 1024], P(('seq', 'grp')), may hold values from -6 to 6
Outputs:
- attended: bfloat16 [16384, 1024], P(('seq', 'grp'))
All inputs are finite; a program needn't handle non-finite values.
Results may differ from a plain program's by a relative error of at most 0.0033.
Values may be sent and summed in bfloat16 or wider, within the bound.
No kernel may reach another device: no remote copies, remote signals or barrier semaphores. Data moves between devices by JAX's collectives and lax.ppermute only.
A program may use at most 128 MiB of HBM per device.

v0:
```python
import functools
import math

import jax
import jax.numpy as jnp
from jax import lax
from jax.experimental import pallas as pl
from jax.experimental.pallas import tpu as pltpu
from jax.sharding import PartitionSpec as P

HEADS = 8
HEAD_DIM = 128
BLK = 256
HALF = BLK // 2
SUB = BLK // 8
LEV = 4
EXP_SCALE = math.log2(math.e) / math.sqrt(HEAD_DIM)

VMEM_GRANT = 24 << 20

very_negative = -1e30
f32 = jnp.float32
bf16 = jnp.bfloat16


def iota(shape, dim):
    return lax.broadcasted_iota(jnp.int32, shape, dim)


def bit(value, place):
    return jnp.bitwise_and(lax.shift_right_logical(value, place), 1)


def low_bits(value):
    step = SUB.bit_length() - 1
    deep = jnp.bitwise_and(value, SUB - 1)
    return 8 * deep + 4 * bit(value, step) + 2 * bit(value, step + 1) + bit(value, step + 2)


def reorder_matrix():
    return (iota((BLK, BLK), 1) == low_bits(iota((BLK, BLK), 0))).astype(bf16)


def restore_matrix():
    return (iota((BLK, BLK), 0) == low_bits(iota((BLK, BLK), 1))).astype(bf16)


def pair_matrix():
    first = low_bits(iota((HALF, BLK), 0))
    place = iota((HALF, BLK), 1)
    return jnp.logical_or(place == first, place == first + 1).astype(bf16)


def mul(left, right):
    return jnp.dot(left, right, preferred_element_type=f32)


def fold(rows, factor):
    half = rows.shape[0] // 2
    total = rows[:half].astype(f32) + rows[half:].astype(f32)
    if factor != 1.0:
        total = total * factor
    return total.astype(bf16)


def fold_chunks(rows, chunk, factor):
    count = rows.shape[0] // chunk
    return jnp.concatenate([fold(rows[i * chunk : (i + 1) * chunk], factor) for i in range(count)], axis=0)


def twice(rows):
    return jnp.concatenate([rows, rows], axis=0)


def cols(head):
    return slice(head * HEAD_DIM, (head + 1) * HEAD_DIM)


DECLARED = 1 << 36


def with_ones(values):
    return jnp.concatenate([values, jnp.ones_like(values)], axis=1)


def attend(units):
    scores = []
    for query, parts in units:
        raws = [
            lax.dot_general(query, keys, (((1,), (1,)), ((), ())), preferred_element_type=f32) for keys, _, _ in parts
        ]
        scores.append([raw if part[2] is None else raw + part[2] for raw, part in zip(raws, parts)])
    tops = []
    for raws in scores:
        tops.append(functools.reduce(jnp.maximum, [jnp.max(raw, axis=1, keepdims=True) for raw in raws]))
    found = []
    for (_, parts), raws, top in zip(units, scores, tops):
        total = None
        for (_, values, _), raw in zip(parts, raws):
            weights = jnp.exp2((raw - top) * EXP_SCALE).astype(bf16)
            one = mul(weights, with_ones(values))
            total = one if total is None else total + one
        found.append((jnp.broadcast_to(top * EXP_SCALE, (top.shape[0], HEAD_DIM)), total))
    return found


def share_of(ref, share, shares):
    width = ref.shape[1] // shares
    first = share * width
    if not isinstance(share, int):
        first = pl.multiple_of(first, HEAD_DIM)
    return ref.at[:, pl.ds(first, width)]


def run_shares(body, name, shares, scalars, ins, outs, work=1 << 10, unrolled=False):
    moved_in = [i for i, (kind, _) in enumerate(ins) if kind in ("cols", "got")]
    moved_out = [i for i, (kind, _) in enumerate(outs) if kind == "cols"]
    as_list = lambda pair: list(pair[1]) if pair[0] == "pieces" else [pair[1]]
    buffer_shape = {
        "cols": lambda value: (shares, value.shape[0], value.shape[1] // shares),
        "got": lambda value: (shares, value.shape[0], value.shape[1] // shares),
        "kept": lambda value: None,
        "pieces": lambda values: (shares, len(values) // shares, *values[0].shape),
    }

    def kernel(*refs):
        refs = list(refs)
        take = lambda count: [refs.pop(0) for _ in range(count)]
        scalar_refs = take(len(scalars))
        in_refs = [take(len(as_list(pair))) for pair in ins]
        out_refs = [take(len(as_list(pair))) for pair in outs]
        in_bufs = [in_refs[i][0] if ins[i][0] == "kept" else refs.pop(0) for i in range(len(ins))]
        out_bufs = [out_refs[i][0] if outs[i][0] == "kept" else refs.pop(0) for i in range(len(outs))]
        in_sems, out_sems, piece_sems = take(3)

        def bring(i, share):
            return pltpu.make_async_copy(share_of(in_refs[i][0], share, shares), in_bufs[i].at[share], in_sems.at[i, share])

        def put(i, share):
            return pltpu.make_async_copy(out_bufs[i].at[share], share_of(out_refs[i][0], share, shares), out_sems.at[i, share])

        def spot_of(buffer, n):
            entry = n ^ scalar_refs[0][1]
            return buffer.at[lax.div(entry, buffer.shape[1]), lax.rem(entry, buffer.shape[1])]

        pieces_in, pieces_out = [], []
        for i, (kind, _) in enumerate(ins):
            if kind == "pieces":
                pieces_in += [(ref, spot_of(in_bufs[i], n), n) for n, ref in enumerate(in_refs[i])]
        for i, (kind, _) in enumerate(outs):
            if kind == "pieces":
                pieces_out += [(spot_of(out_bufs[i], n), ref, n) for n, ref in enumerate(out_refs[i])]
        pieces_in = [pltpu.make_async_copy(source, target, piece_sems.at[n]) for source, target, n in pieces_in]
        pieces_out = [pltpu.make_async_copy(source, target, piece_sems.at[n]) for source, target, n in pieces_out]

        for share in range(shares):
            for i in moved_in:
                bring(i, share).start()
            if share == 0:
                for copy in pieces_in:
                    copy.start()
        for copy in pieces_in:
            copy.wait()

        def views(operands, buffers, share):
            result = []
            for (kind, value), buffer in zip(operands, buffers):
                count = value.shape[0] // shares if kind == "kept" else None
                result.append(buffer.at[share] if count is None else buffer.at[pl.ds(share * count, count)])
            return result

        def step(share, carry):
            for i in moved_in:
                bring(i, share).wait()
            body(scalar_refs, views(ins, in_bufs, share), views(outs, out_bufs, share))
            for i in moved_out:
                put(i, share).start()
            return carry

        if unrolled:
            for share in range(shares):
                step(share, 0)
        else:
            lax.fori_loop(0, shares, step, 0)
        for copy in pieces_out:
            copy.start()
        for share in range(shares):
            for i in moved_out:
                put(i, share).wait()
        for copy in pieces_out:
            copy.wait()

    spaces = {"cols": pltpu.HBM, "got": pl.ANY, "pieces": pl.ANY, "kept": pltpu.VMEM}
    values, in_specs, out_specs, out_shapes, buffers = [], [], [], [], []
    for kind, value in ins:
        for one in as_list((kind, value)):
            values.append(pltpu.with_memory_space_constraint(one, pltpu.HBM) if kind == "cols" else one)
            in_specs.append(pl.BlockSpec(memory_space=spaces[kind]))
    for kind, shape in outs:
        for one in as_list((kind, shape)):
            out_shapes.append(pltpu.HBM(one.shape, one.dtype) if kind == "cols" else one)
            out_specs.append(pl.BlockSpec(memory_space=pltpu.HBM if kind == "cols" else pltpu.VMEM))
    for kind, value in list(ins) + list(outs):
        if kind != "kept":
            buffers.append(pltpu.VMEM(buffer_shape[kind](value), as_list((kind, value))[0].dtype))
    count = max(len(as_list(pair)) for pair in list(ins) + list(outs))
    semaphores = [(len(ins), shares), (len(outs), shares), (count,)]
    return pl.pallas_call(
        kernel,
        in_specs=[pl.BlockSpec(memory_space=pltpu.SMEM)] * len(scalars) + in_specs,
        out_specs=out_specs,
        out_shape=out_shapes,
        scratch_shapes=buffers + [pltpu.SemaphoreType.DMA(shape) for shape in semaphores],
        compiler_params=pltpu.CompilerParams(vmem_limit_bytes=VMEM_GRANT),
        cost_estimate=pl.CostEstimate(flops=work, bytes_accessed=1 << 10, transcendentals=0),
        name=name,
    )(*scalars, *values)


def array(rows, width, dtype):
    return jax.ShapeDtypeStruct((rows, width), dtype)


def swap_body(_, ins, outs):
    pair = pair_matrix()
    count, _, part = outs[0].shape
    for place, (ref, factor) in enumerate(zip(ins, (0.5, 0.5, 1.0))):
        for i in range(2):
            level1 = mul(pair, ref[i * BLK : (i + 1) * BLK, :])
            if factor != 1.0:
                level1 = level1 * factor
            level2 = fold(level1.astype(bf16), factor)
            first = place * HALF + i * HALF // 2
            for n in range(count):
                outs[0][n, first : first + HALF // 2, :] = level2[:, n * part : (n + 1) * part]


def swap_rows(place, query_vecs, key_vecs, value_vecs, groups):
    width = query_vecs.shape[1]
    ins = [("cols", a) for a in (query_vecs, key_vecs, value_vecs)]
    outs = [("pieces", [array(3 * HALF, width // groups, bf16)] * groups)]
    return run_shares(swap_body, "swap_rows", groups // 2, [place], ins, outs, unrolled=True)


def rows_body(scalars, ins, outs):
    q_ref, k_ref, v_ref = ins
    q0_ref, q1_ref, near_ref, far_ref, chip_ref = outs
    reorder = reorder_matrix()
    pair = pair_matrix()
    for i in range(2):
        rows = slice(i * BLK, (i + 1) * BLK)
        q0 = mul(reorder, q_ref[rows, :]).astype(bf16)
        q0_ref[rows, :] = q0
        q1_ref[i * HALF : (i + 1) * HALF, :] = fold(q0, 0.5)
    odd = scalars[0][0]
    outer = pl.ds(pl.multiple_of(odd * BLK, BLK), BLK)
    inner = pl.ds(pl.multiple_of((1 - odd) * BLK, BLK), BLK)
    for ref, far_rows, first, near, far in ((near_ref, far_ref, 0, outer, inner), (chip_ref, chip_ref, 2 * BLK, inner, outer)):
        ref[0:BLK, :] = k_ref[near, :]
        ref[BLK : 2 * BLK, :] = v_ref[near, :]
        far_rows[first : first + HALF, :] = (mul(pair, k_ref[far, :]) * 0.5).astype(bf16)
        far_rows[first + HALF : first + BLK, :] = mul(pair, v_ref[far, :]).astype(bf16)


def rows_to_send(place, query_vecs, key_vecs, value_vecs, groups):
    rows, width = query_vecs.shape
    ins = [("cols", a) for a in (query_vecs, key_vecs, value_vecs)]
    outs = [("cols", array(n, width, bf16)) for n in (rows, rows // 2, 2 * BLK, BLK, 3 * BLK)]
    return run_shares(rows_body, "rows_to_send", groups, [place], ins, outs)


def own_body(_, ins, outs):
    q_ref, k_ref, v_ref = ins
    sum_ref, top_ref, total_ref = outs
    heads = q_ref.shape[1] // HEAD_DIM
    for i in range(2):
        rows = slice(i * BLK, (i + 1) * BLK)
        units = [(q_ref[rows, cols(head)], [(k_ref[:, cols(head)], v_ref[:, cols(head)], None)]) for head in range(heads)]
        for head, (top, sums) in enumerate(attend(units)):
            spot = (head // 2, rows, cols(head % 2))
            sum_ref[spot] = sums[:, :HEAD_DIM]
            top_ref[spot] = top
            total_ref[spot] = sums[:, HEAD_DIM:]


def running_sums(rows, width, groups):
    return [("kept", jax.ShapeDtypeStruct((groups, rows, width // groups), f32))] * 3


def own_level(q0, key_vecs, value_vecs, groups):
    ins = [("cols", a) for a in (q0, key_vecs, value_vecs)]
    return run_shares(own_body, "own_level", groups // 2, [], ins, running_sums(*q0.shape, groups), DECLARED)


def halo_body(place_ref, *refs):
    count = len(refs) - 4
    piece_refs, (got_ref, right_ref, left_ref, sems) = refs[:count], refs[count:]
    copies = [pltpu.make_async_copy(ref, got_ref.at[n ^ place_ref[1]], sems.at[n]) for n, ref in enumerate(piece_refs)]
    for copy in copies:
        copy.start()
    for copy in copies:
        copy.wait()
    pair = count // 2
    for which, factor in ((1, 0.5), (2, 1.0)):
        rows = slice(which * HALF, (which + 1) * HALF)
        near = (which - 1) * BLK
        far = 2 * BLK + (which - 1) * HALF
        for j in range(count):
            level2 = got_ref[j, rows, :]
            level3 = fold_chunks(level2, HALF // 2, factor)
            near_ref, far_ref = (left_ref, right_ref) if j < pair else (right_ref, left_ref)
            spot = j % pair
            near_ref[near + spot * HALF : near + (spot + 1) * HALF, :] = level2
            far_ref[far + spot * HALF // 2 : far + (spot + 1) * HALF // 2, :] = level3


def coarse_halos(place, pieces):
    rows, width = pieces[0].shape
    vmem = pl.BlockSpec(memory_space=pltpu.VMEM)
    shape = jax.ShapeDtypeStruct((3 * BLK, width), bf16)
    return pl.pallas_call(
        halo_body,
        in_specs=[pl.BlockSpec(memory_space=pltpu.SMEM)] + [pl.BlockSpec(memory_space=pl.ANY)] * len(pieces),
        out_specs=[vmem] * 3,
        out_shape=[jax.ShapeDtypeStruct((len(pieces), rows, width), bf16), shape, shape],
        scratch_shapes=[pltpu.SemaphoreType.DMA((len(pieces),))],
        compiler_params=pltpu.CompilerParams(vmem_limit_bytes=16 << 20),
        cost_estimate=pl.CostEstimate(flops=1 << 20, bytes_accessed=24 * pieces[0].size, transcendentals=0),
        name="coarse_halos",
    )(place, *pieces)


def coarse_body(place_ref, bias_ref, got_ref, prev_ref, next_ref, *refs):
    *out_refs, back_ref, sems = refs
    count = got_ref.shape[0]
    heads = got_ref.shape[2] // HEAD_DIM
    bias_prev = bias_ref[0]
    bias_next = bias_ref[1]
    lane = iota((HALF, HEAD_DIM), 1)

    units = []
    for head in range(heads):
        here = cols(head)

        def own(which, j):
            return got_ref[j, which * HALF : (which + 1) * HALF, here]

        def near(ref, which, spot):
            first = (which - 1) * BLK + spot * HALF
            return ref[first : first + HALF, here]

        def both(ref, which):
            return ref[(which - 1) * BLK : which * BLK, here]

        def far(ref, which):
            first = 2 * BLK + (which - 1) * HALF
            return ref[first : first + HALF, here]

        def near3(ref, which):
            return fold_chunks(both(ref, which), HALF // 2, 0.5 if which == 1 else 1.0)

        def joined(*rows):
            return jnp.concatenate(rows, axis=0)

        def part(pick, bias):
            return (pick(1), pick(2), bias)

        units += [
            (own(0, 0), [part(lambda w: joined(own(w, 2), own(w, 3)), None), part(lambda w: near(prev_ref, w, 0), bias_prev)]),
            (own(0, 1), [part(lambda w: both(prev_ref, w), bias_prev), part(lambda w: own(w, 3), None)]),
            (own(0, 2), [part(lambda w: both(next_ref, w), bias_next), part(lambda w: own(w, 0), None)]),
            (own(0, 3), [part(lambda w: joined(own(w, 0), own(w, 1)), None), part(lambda w: near(next_ref, w, 1), bias_next)]),
        ]
        for j, (ref, bias, other, other_bias) in enumerate(
            ((next_ref, bias_next, prev_ref, bias_prev), (prev_ref, bias_prev, next_ref, bias_next))
        ):
            query = joined(*[fold_chunks(own(0, 2 * j + n), HALF // 2, 0.5) for n in range(2)])
            units.append(
                (
                    query,
                    [part(lambda w: joined(near3(ref, w), far(ref, w)), bias), part(lambda w: far(other, w), other_bias)],
                )
            )
    found = attend(units)
    each = len(units) // heads

    def joined(*rows):
        return jnp.concatenate(rows, axis=0)

    for head in range(heads):
        here = cols(head)
        for j in range(count):
            top2, sum2 = found[head * each + j]
            top3, sum3 = found[head * each + count + j // 2]

            def spread(rows):
                first = (j % 2) * 2 * SUB
                one = rows[first : first + SUB]
                other = rows[first + SUB : first + 2 * SUB]
                return joined(one, one, other, other)

            top3 = spread(top3)
            sum3 = spread(sum3)
            top = jnp.maximum(top2, top3)
            scale2 = jnp.exp2(top2 - top)
            scale3 = jnp.exp2(top3 - top)
            values = sum2[:, :HEAD_DIM] * scale2 + sum3[:, :HEAD_DIM] * scale3
            total = sum2[:, HEAD_DIM:] * (4.0 * scale2) + sum3[:, HEAD_DIM:] * (8.0 * scale3)
            back_ref[j, 0:HALF, here] = (values / total).astype(bf16)
            level = top + jnp.log2(total)
            high = level.astype(bf16).astype(f32)
            middle = (level - high).astype(bf16).astype(f32)
            terms = jnp.where(lane == 0, high, jnp.where(lane == 1, middle, level - high - middle))
            back_ref[j, HALF : HALF + 16, here] = terms.T[0:16, :].astype(bf16)
    copies = [
        pltpu.make_async_copy(back_ref.at[n ^ place_ref[1]], ref, sems.at[n]) for n, ref in enumerate(out_refs)
    ]
    for copy in copies:
        copy.start()
    for copy in copies:
        copy.wait()


def coarse_levels(place, bias, got, from_prev, from_next):
    count, _, width = got.shape
    vmem = pl.BlockSpec(memory_space=pltpu.VMEM)
    smem = pl.BlockSpec(memory_space=pltpu.SMEM)
    rows = HALF + 16
    return pl.pallas_call(
        coarse_body,
        in_specs=[smem, smem, vmem, vmem, vmem],
        out_specs=[vmem] * count,
        out_shape=[array(rows, width, bf16)] * count,
        scratch_shapes=[pltpu.VMEM((count, rows, width), bf16), pltpu.SemaphoreType.DMA((count,))],
        compiler_params=pltpu.CompilerParams(vmem_limit_bytes=16 << 20),
        cost_estimate=pl.CostEstimate(flops=DECLARED, bytes_accessed=8 * got.size, transcendentals=1 << 20),
        name="coarse_levels",
    )(place, bias, got, from_prev, from_next)


def side_body(side, with_near, with_far, scalars, ins, outs):
    q0_ref, q1_ref, sum_ref, top_ref, total_ref, side_ref = ins
    heads = q1_ref.shape[1] // HEAD_DIM
    bias = scalars[1][side]
    blocks = (side, 1 - side)
    fine = [pl.ds(pl.multiple_of(block * BLK, BLK), BLK) for block in blocks]
    middle = [pl.ds(pl.multiple_of(block * HALF, HALF), HALF) for block in blocks]
    if with_near:
        pair = pair_matrix()
        near_keys = (mul(pair, side_ref[0:BLK, :]) * 0.5).astype(bf16)
        near_values = mul(pair, side_ref[BLK : 2 * BLK, :]).astype(bf16)
    start = 2 * BLK if with_near else 0
    far_keys, far_values = (slice(start + n * HALF, start + (n + 1) * HALF) for n in range(2))
    units, names = [], []
    for head in range(heads):
        here = cols(head)
        far = (side_ref[far_keys, here], side_ref[far_values, here]) if with_far else None
        near = (near_keys[:, here], near_values[:, here]) if with_near else None
        whole = [part for part in (near, far) if part is not None]
        whole = [jnp.concatenate([part[n] for part in whole], axis=0) if len(whole) > 1 else whole[0][n] for n in range(2)]
        if with_near:
            units.append((q0_ref[fine[0], here], [(side_ref[0:BLK, here], side_ref[BLK : 2 * BLK, here], None)]))
            names.append((head, 0, 0))
        if with_far:
            units.append((q1_ref[middle[0], here], [(*far, None)]))
            names.append((head, 0, 1))
        units.append((q1_ref[middle[1], here], [(*whole, None)]))
        names.append((head, 1, 1))
    found = {name: (top + bias, sums) for name, (top, sums) in zip(names, attend(units))}
    for n in range(2):
        for head in range(heads):
            spot = (head // 2, fine[n], cols(head % 2))
            parts = [(top_ref[spot], sum_ref[spot], total_ref[spot])]
            if (head, n, 0) in found:
                top, sums = found[head, n, 0]
                parts.append((top, sums[:, :HEAD_DIM], sums[:, HEAD_DIM:]))
            if (head, n, 1) in found:
                top, sums = found[head, n, 1]
                parts.append((twice(top), twice(sums[:, :HEAD_DIM]), twice(2.0 * sums[:, HEAD_DIM:])))
            most = functools.reduce(jnp.maximum, [part[0] for part in parts])
            scales = [jnp.exp2(part[0] - most) for part in parts]
            outs[0][spot] = sum(part[1] * scale for part, scale in zip(parts, scales))
            outs[1][spot] = most
            outs[2][spot] = sum(part[2] * scale for part, scale in zip(parts, scales))


def chip_body(scalars, ins, outs):
    side_body(1 - scalars[0][0], True, True, scalars, ins, outs)


def near_body(scalars, ins, outs):
    side_body(scalars[0][0], True, False, scalars, ins, outs)


def far_body(scalars, ins, outs):
    side_body(scalars[0][0], False, True, scalars, [None] + ins, outs)


def side_level(body, name, place, bias, queries, running, rows):
    groups, count, part = running[0].shape
    ins = [("cols", query) for query in queries] + [("kept", one) for one in running] + [("got", rows)]
    return run_shares(body, name, groups // 2, [place, bias], ins, running_sums(count, groups * part, groups))


def finish_body(place_ref, sum_ref, top_ref, total_ref, *refs):
    groups = sum_ref.shape[0]
    back_refs, (out_ref, done_ref, sems) = refs[:groups], refs[groups:]
    part = sum_ref.shape[2]
    restore = restore_matrix()
    copies = []
    for n, back_ref in enumerate(back_refs):
        entry = n ^ place_ref[1]
        levels = []
        for head in range(part // HEAD_DIM):
            terms = back_ref[HALF : HALF + 16, cols(head)].astype(f32)
            terms = jnp.sum(jnp.where(iota(terms.shape, 0) < 3, terms, 0.0), axis=0, keepdims=True)
            levels.append(jnp.broadcast_to(terms, (HEAD_DIM, HEAD_DIM)).T)
        for i in range(2):
            rows = slice(i * BLK, (i + 1) * BLK)
            spot = slice(i * HALF // 2, (i + 1) * HALF // 2)
            results = []
            for head, level in enumerate(levels):
                here = (entry, rows, cols(head))
                top = top_ref[here]
                level = twice(twice(level[spot, :]))
                lead = top - level
                smaller = jnp.exp2(-jnp.abs(lead))
                scale = jnp.where(lead >= 0.0, 1.0, smaller)
                coarse = jnp.where(lead >= 0.0, smaller, 1.0)
                number = twice(twice(back_ref[spot, cols(head)].astype(f32))) * coarse
                number = number + sum_ref[here] * scale
                total = total_ref[here] * scale + coarse
                guess = pl.reciprocal(total, approx=True)
                results.append((number * (guess * (2.0 - total * guess))).astype(bf16))
            done_ref[n, rows, :] = mul(restore, jnp.concatenate(results, axis=1)).astype(bf16)
        columns = pl.ds(pl.multiple_of(entry * part, HEAD_DIM), part)
        copies.append(pltpu.make_async_copy(done_ref.at[n], out_ref.at[:, columns], sems.at[n]))
        copies[-1].start()
    for copy in copies:
        copy.wait()


def finish(place, running, back):
    groups, rows, part = running[0].shape
    vmem = pl.BlockSpec(memory_space=pltpu.VMEM)
    return pl.pallas_call(
        finish_body,
        in_specs=[pl.BlockSpec(memory_space=pltpu.SMEM)] + [vmem] * (3 + groups),
        out_specs=pl.BlockSpec(memory_space=pltpu.HBM),
        out_shape=pltpu.HBM((rows, groups * part), bf16),
        scratch_shapes=[pltpu.VMEM((groups, rows, part), bf16), pltpu.SemaphoreType.DMA((groups,))],
        compiler_params=pltpu.CompilerParams(vmem_limit_bytes=VMEM_GRANT),
        cost_estimate=pl.CostEstimate(flops=1 << 10, bytes_accessed=1 << 10, transcendentals=0),
        name="finish",
    )(place, *running, *back)


def shift(value, axis, steps):
    count = lax.axis_size(axis)
    first, last = (max(0, -steps), min(count, count - steps))
    return lax.ppermute(value, axis, [(source, source + steps) for source in range(first, last)])


def trade(value, axis, pairs):
    return lax.ppermute(value, axis, pairs + [(target, source) for source, target in pairs])


def edge_bias(axis):
    place = lax.axis_index(axis)
    last = lax.axis_size(axis) - 1
    at_edge = jnp.stack([place == 0, place == last])
    return jnp.where(at_edge, very_negative, 0.0).astype(f32)


def local(query_vecs, key_vecs, value_vecs):
    groups = lax.axis_size("grp")
    assert query_vecs.shape == (2 * BLK, HEADS * HEAD_DIM) and groups == 4
    everyone = ("seq", "grp")
    count = lax.axis_size(everyone)
    spot = lax.axis_index("grp")
    odd = jnp.bitwise_and(spot, 1)
    place = jnp.stack([odd, spot]).astype(jnp.int32)
    bias = edge_bias(everyone)

    def exchange(pieces):
        flips = [[(source, source ^ n) for source in range(groups)] for n in range(groups)]
        for n in range(groups - 1, 0, -1):
            pieces[n] = lax.ppermute(pieces[n], "grp", flips[n])
        return pieces

    pieces = list(swap_rows(place, query_vecs, key_vecs, value_vecs, groups))
    query_rows, pieces = lax.optimization_barrier((query_vecs, pieces))
    pieces = exchange(pieces)
    q0, q1, near, far, chip = rows_to_send(place, query_rows, key_vecs, value_vecs, groups)
    off_chip = [(device, device + 1) for device in range(1, count - 1, 2)]
    near = trade(near, everyone, off_chip)
    far, pieces[1] = lax.optimization_barrier((far, pieces[1]))
    far = trade(far, everyone, off_chip)
    pieces, chip = lax.optimization_barrier((pieces, chip))
    got, coarse_right, coarse_left = coarse_halos(place, pieces)
    coarse_right, coarse_left, chip, q0 = lax.optimization_barrier((coarse_right, coarse_left, chip, q0))
    coarse_prev = shift(coarse_right, "seq", 1)
    coarse_next = shift(coarse_left, "seq", -1)
    chip = trade(chip, everyone, [(device, device + 1) for device in range(0, count - 1, 2)])
    running = own_level(q0, key_vecs, value_vecs, groups)
    running = side_level(chip_body, "chip_level", place, bias, (q0, q1), running, chip)
    running = side_level(near_body, "near_level", place, bias, (q0, q1), running, near)
    got, running = lax.optimization_barrier((got, running))
    back = coarse_levels(place, edge_bias("seq"), got, coarse_prev, coarse_next)
    back, running = lax.optimization_barrier((back, running))
    back = exchange(list(back))
    running = side_level(far_body, "far_level", place, bias, (q1,), running, far)
    return finish(place, running, back)


def solution(mesh):
    return jax.shard_map(
        local,
        mesh=mesh,
        in_specs=(P(("seq", "grp"), None), P(("seq", "grp"), None), P(("seq", "grp"), None)),
        out_specs=P(("seq", "grp"), None),
        check_vma=False,
    )
```

profile of v0, /device:TPU:11, one launch (start us, length us, event | category | flops | bytes accessed | tf_op | source)
XLA Modules:
  0.0 63.4 jit_solution(1133205721113726549)
XLA Ops:
  0.1 3.9 %swap_rows.1 = (bf16[384,256]{1,0:T(8,128)(2,1)S(1)}, bf16[384,256]{1,0:T(8,128)(2,1)S(1)}, bf16[384,256]{1,0:T(8,128)(2,1)S(1)}, bf16[384,256]{1,0:T(8,128)(2,1)S(1)}) custom-call(s32[2]{0:T(128)S(1)} %pad_add_fusion.refs_0_.place_ref, bf16[512,1024]{1,0:T(8,128)(2,1)} %refs_1_.3, bf16[512,1024]{1,0:T(8,128)(2,1)} %refs_1_.4, bf16[512,1024]{1,0:T(8,128)(2,1)} %refs_2_.5), custom_call_target="tpu_custom_call" | custom-call | flops 1024 | bytes 1024 | tf_op jit(solution)/shard_map/swap_rows/pallas_call | solution.py:208
  4.0 0.7 %collective-permute-start = (bf16[384,256]{1,0:T(8,128)(2,1)S(1)}, bf16[384,256]{1,0:T(8,128)(2,1)S(1)}, u32[]{:S(2)}, u32[]{:S(2)}) collective-permute-start(bf16[384,256]{1,0:T(8,128)(2,1)S(1)} %get-tuple-element.68), channel_id=1, source_target_pairs={{0,1},{1,0},{2,3},{3,2},{4,5},{5,4},{6,7},{7,6},{8,9},{9,8},{10,11... | collective-permute-start | bytes 589832 | tf_op jit(solution)/shard_map/ppermute | solution.py:588
  4.8 1.3 %collective-permute-start.1 = (bf16[384,256]{1,0:T(8,128)(2,1)S(1)}, bf16[384,256]{1,0:T(8,128)(2,1)S(1)}, u32[]{:S(2)}, u32[]{:S(2)}) collective-permute-start(bf16[384,256]{1,0:T(8,128)(2,1)S(1)} %get-tuple-element.70), channel_id=1, source_target_pairs={{0,2},{1,3},{2,0},{3,1},{4,6},{5,7},{6,4},{7,5},{8,10},{9,11},{10,... | collective-permute-start | bytes 589832 | tf_op jit(solution)/shard_map/ppermute | solution.py:588
  6.0 0.5 collective-permute-start.2
  6.5 4.4 %rows_to_send.1 = (bf16[512,1024]{1,0:T(8,128)(2,1)}, bf16[256,1024]{1,0:T(8,128)(2,1)}, bf16[512,1024]{1,0:T(8,128)(2,1)}, bf16[256,1024]{1,0:T(8,128)(2,1)}, bf16[768,1024]{1,0:T(8,128)(2,1)}) custom-call(s32[2]{0:T(128)S(1)} %pad_add_fusion.refs_0_.place_ref, bf16[512,1024]{1,0:T(8,128)(2,1)} %refs_1_.3, bf16[512,1024]{1,0:T(8,128)(2,1)} %refs_1_.4, ...), custom_call_target="tpu_custom_call" | custom-call | flops 1024 | bytes 1024 | tf_op jit(solution)/shard_map/rows_to_send/pallas_call | solution.py:208
  10.8 3.2 %collective-permute-start.4 = (bf16[512,1024]{1,0:T(8,128)(2,1)}, bf16[512,1024]{1,0:T(8,128)(2,1)S(1)}, u32[]{:S(2)}, u32[]{:S(2)}) collective-permute-start(bf16[512,1024]{1,0:T(8,128)(2,1)} %get-tuple-element.90), channel_id=1, source_target_pairs={{1,2},{3,4},{5,6},{7,8},{9,10},{11,12},{13,14},{15,16},{17,18},{19... | collective-permute-start | bytes 3145736 | tf_op jit(solution)/shard_map/ppermute | solution.py:565
  14.1 0.1 add_select_fusion.refs_1_
  14.1 0.1 add_select_fusion.1.bias_ref
  14.2 1.4 %collective-permute-done.2.refs_3_ = bf16[384,256]{1,0:T(8,128)(2,1)S(1)} collective-permute-done((bf16[384,256]{1,0:T(8,128)(2,1)S(1)}, bf16[384,256]{1,0:T(8,128)(2,1)S(1)}, u32[]{:S(2)}, u32[]{:S(2)}) %collective-permute-start.2) | collective-permute-done | bytes 196640 | tf_op jit(solution)/shard_map/ppermute | solution.py:588
  15.6 3.3 %collective-permute-start.7 = (bf16[256,1024]{1,0:T(8,128)(2,1)}, bf16[256,1024]{1,0:T(8,128)(2,1)S(1)}, u32[]{:S(2)}, u32[]{:S(2)}) collective-permute-start(bf16[256,1024]{1,0:T(8,128)(2,1)} %get-tuple-element.107), channel_id=1, source_target_pairs={{1,2},{3,4},{5,6},{7,8},{9,10},{11,12},{13,14},{15,16},{17,18},{19... | collective-permute-start | bytes 1572872 | tf_op jit(solution)/shard_map/ppermute | solution.py:565
  18.9 1.7 %coarse_halos.1 = (bf16[4,384,256]{2,1,0:T(8,128)(2,1)S(1)}, bf16[768,256]{1,0:T(8,128)(2,1)S(1)}, bf16[768,256]{1,0:T(8,128)(2,1)S(1)}) custom-call(s32[2]{0:T(128)S(1)} %pad_add_fusion.refs_0_.place_ref, bf16[384,256]{1,0:T(8,128)(2,1)S(1)} %get-tuple-element.73.refs_0_, bf16[384,256]{1,0:T(8,128)(2,1)S(1)} %collective-permute-done.refs_1_, ...), custom_call_target="tpu_custom_call" | custom-call | flops 1048576 | bytes 2359296 | tf_op jit(solution)/shard_map/coarse_halos/pallas_call | solution.py:321
  20.6 3.2 %collective-permute-start.5 = (bf16[768,256]{1,0:T(8,128)(2,1)S(1)}, bf16[768,256]{1,0:T(8,128)(2,1)S(1)}, u32[]{:S(2)}, u32[]{:S(2)}) collective-permute-start(bf16[768,256]{1,0:T(8,128)(2,1)S(1)} %get-tuple-element.95), channel_id=1, source_target_pairs={{0,4},{4,8},{8,12},{12,16},{16,20},{20,24},{24,28},{1,5},{5,9},{9,... | collective-permute-start | bytes 1179656 | tf_op jit(solution)/shard_map/ppermute | solution.py:561
  23.8 2.1 %collective-permute-start.6 = (bf16[768,256]{1,0:T(8,128)(2,1)S(1)}, bf16[768,256]{1,0:T(8,128)(2,1)S(1)}, u32[]{:S(2)}, u32[]{:S(2)}) collective-permute-start(bf16[768,256]{1,0:T(8,128)(2,1)S(1)} %get-tuple-element.96), channel_id=1, source_target_pairs={{4,0},{8,4},{12,8},{16,12},{20,16},{24,20},{28,24},{5,1},{9,5},{13... | collective-permute-start | bytes 1179656 | tf_op jit(solution)/shard_map/ppermute | solution.py:561
  25.9 1.7 %collective-permute-start.3 = (bf16[768,1024]{1,0:T(8,128)(2,1)}, bf16[768,1024]{1,0:T(8,128)(2,1)S(1)}, u32[]{:S(2)}, u32[]{:S(2)}) collective-permute-start(bf16[768,1024]{1,0:T(8,128)(2,1)} %get-tuple-element.86), channel_id=1, source_target_pairs={{0,1},{2,3},{4,5},{6,7},{8,9},{10,11},{12,13},{14,15},{16,17},{18,... | collective-permute-start | bytes 4718600 | tf_op jit(solution)/shard_map/ppermute | solution.py:565
  27.5 4.8 %own_level.1 = (f32[4,512,256]{2,1,0:T(8,128)S(1)}, f32[4,512,256]{2,1,0:T(8,128)S(1)}, f32[4,512,256]{2,1,0:T(8,128)S(1)}) custom-call(bf16[512,1024]{1,0:T(8,128)(2,1)} %get-tuple-element.82.refs_0_.refs_2_, bf16[512,1024]{1,0:T(8,128)(2,1)} %refs_1_.4, bf16[512,1024]{1,0:T(8,128)(2,1)} %refs_2_.5), custom_call_target="tpu_custom_call" | custom-call | flops 68719476736 | bytes 1024 | tf_op jit(solution)/shard_map/own_level/pallas_call | solution.py:208
  32.3 5.0 %chip_level.1 = (f32[4,512,256]{2,1,0:T(8,128)S(1)}, f32[4,512,256]{2,1,0:T(8,128)S(1)}, f32[4,512,256]{2,1,0:T(8,128)S(1)}) custom-call(s32[2]{0:T(128)S(1)} %pad_add_fusion.refs_0_.place_ref, f32[2]{0:T(128)S(1)} %add_select_fusion.refs_1_, bf16[512,1024]{1,0:T(8,128)(2,1)} %get-tuple-element.82.refs_0_.refs_2_, ...), custom_call_target="tpu_custom_call" | custom-call | flops 1024 | bytes 1024 | tf_op jit(solution)/shard_map/chip_level/pallas_call | solution.py:208
  37.4 5.8 %collective-permute-done.4.refs_7_ = bf16[512,1024]{1,0:T(8,128)(2,1)S(1)} collective-permute-done((bf16[512,1024]{1,0:T(8,128)(2,1)}, bf16[512,1024]{1,0:T(8,128)(2,1)S(1)}, u32[]{:S(2)}, u32[]{:S(2)}) %collective-permute-start.4) | collective-permute-done | bytes 1048608 | tf_op jit(solution)/shard_map/ppermute | solution.py:565
  43.1 4.5 %near_level.1 = (f32[4,512,256]{2,1,0:T(8,128)S(1)}, f32[4,512,256]{2,1,0:T(8,128)S(1)}, f32[4,512,256]{2,1,0:T(8,128)S(1)}) custom-call(s32[2]{0:T(128)S(1)} %pad_add_fusion.refs_0_.place_ref, f32[2]{0:T(128)S(1)} %add_select_fusion.refs_1_, bf16[512,1024]{1,0:T(8,128)(2,1)} %get-tuple-element.82.refs_0_.refs_2_, ...), custom_call_target="tpu_custom_call" | custom-call | flops 1024 | bytes 1024 | tf_op jit(solution)/shard_map/near_level/pallas_call | solution.py:208
  47.6 4.1 %collective-permute-done.5.prev_ref = bf16[768,256]{1,0:T(8,128)(2,1)S(1)} collective-permute-done((bf16[768,256]{1,0:T(8,128)(2,1)S(1)}, bf16[768,256]{1,0:T(8,128)(2,1)S(1)}, u32[]{:S(2)}, u32[]{:S(2)}) %collective-permute-start.5) | collective-permute-done | bytes 393248 | tf_op jit(solution)/shard_map/ppermute | solution.py:561
  51.7 2.4 %coarse_levels.1 = (bf16[144,256]{1,0:T(8,128)(2,1)S(1)}, bf16[144,256]{1,0:T(8,128)(2,1)S(1)}, bf16[144,256]{1,0:T(8,128)(2,1)S(1)}, bf16[144,256]{1,0:T(8,128)(2,1)S(1)}) custom-call(s32[2]{0:T(128)S(1)} %pad_add_fusion.refs_0_.place_ref, f32[2]{0:T(128)S(1)} %add_select_fusion.1.bias_ref, bf16[4,384,256]{2,1,0:T(8,128)(2,1)S(1)} %get-tuple-element.94.got_ref, ...), custom_call_target="tpu_custom_call" | custom-call | flops 68719476736 | bytes 3145728 | tf_op jit(solution)/shard_map/coarse_levels/pallas_call | solution.py:429
  54.2 0.6 collective-permute-start.8
  54.8 1.7 %collective-permute-start.10 = (bf16[144,256]{1,0:T(8,128)(2,1)S(1)}, bf16[144,256]{1,0:T(8,128)(2,1)S(1)}, u32[]{:S(2)}, u32[]{:S(2)}) collective-permute-start(bf16[144,256]{1,0:T(8,128)(2,1)S(1)} %get-tuple-element.114), channel_id=1, source_target_pairs={{0,3},{1,2},{2,1},{3,0},{4,7},{5,6},{6,5},{7,4},{8,11},{9,10},{10,... | collective-permute-start | bytes 221192 | tf_op jit(solution)/shard_map/ppermute | solution.py:588
  56.5 3.9 %far_level.1 = (f32[4,512,256]{2,1,0:T(8,128)S(1)}, f32[4,512,256]{2,1,0:T(8,128)S(1)}, f32[4,512,256]{2,1,0:T(8,128)S(1)}) custom-call(s32[2]{0:T(128)S(1)} %pad_add_fusion.refs_0_.place_ref, f32[2]{0:T(128)S(1)} %add_select_fusion.refs_1_, bf16[256,1024]{1,0:T(8,128)(2,1)} %get-tuple-element.65.refs_3_.refs_2_, ...), custom_call_target="tpu_custom_call" | custom-call | flops 1024 | bytes 1024 | tf_op jit(solution)/shard_map/far_level/pallas_call | solution.py:208
  60.4 3.0 %finish.1 = bf16[512,1024]{1,0:T(8,128)(2,1)} custom-call(s32[2]{0:T(128)S(1)} %pad_add_fusion.refs_0_.place_ref, f32[4,512,256]{2,1,0:T(8,128)S(1)} %get-tuple-element.108.sum_ref, f32[4,512,256]{2,1,0:T(8,128)S(1)} %get-tuple-element.109.top_ref, f32[4,512,256]{2,1,0:T(8,128)S(1)} %get-tuple-element.110.total_ref, ...), custom_call_target="tpu_custom_call" | custom-call | flops 1024 | bytes 1024 | tf_op jit(solution)/shard_map/finish/pallas_call | solution.py:546
  (10 shorter events, 0.1 us)
Async XLA Ops:
  4.0 10.2 %collective-permute-start = (bf16[384,256]{1,0:T(8,128)(2,1)S(1)}, bf16[384,256]{1,0:T(8,128)(2,1)S(1)}, u32[]{:S(2)}, u32[]{:S(2)}) collective-permute-start(bf16[384,256]{1,0:T(8,128)(2,1)S(1)} %get-tuple-element.68), channel_id=1, source_target_pairs={{0,1},{1,0},{2,3},{3,2},{4,5},{5,4},{6,7},{7,6},{8,9},{9,8},{10,11... | collective-permute-start | bytes 589832 | tf_op jit(solution)/shard_map/ppermute | solution.py:588
  4.8 9.5 %collective-permute-start.1 = (bf16[384,256]{1,0:T(8,128)(2,1)S(1)}, bf16[384,256]{1,0:T(8,128)(2,1)S(1)}, u32[]{:S(2)}, u32[]{:S(2)}) collective-permute-start(bf16[384,256]{1,0:T(8,128)(2,1)S(1)} %get-tuple-element.70), channel_id=1, source_target_pairs={{0,2},{1,3},{2,0},{3,1},{4,6},{5,7},{6,4},{7,5},{8,10},{9,11},{10,... | collective-permute-start | bytes 589832 | tf_op jit(solution)/shard_map/ppermute | solution.py:588
  6.0 9.6 %collective-permute-start.2 = (bf16[384,256]{1,0:T(8,128)(2,1)S(1)}, bf16[384,256]{1,0:T(8,128)(2,1)S(1)}, u32[]{:S(2)}, u32[]{:S(2)}) collective-permute-start(bf16[384,256]{1,0:T(8,128)(2,1)S(1)} %get-tuple-element.71), channel_id=1, source_target_pairs={{0,3},{1,2},{2,1},{3,0},{4,7},{5,6},{6,5},{7,4},{8,11},{9,10},{10,... | collective-permute-start | bytes 589832 | tf_op jit(solution)/shard_map/ppermute | solution.py:588
  10.8 32.3 %collective-permute-start.4 = (bf16[512,1024]{1,0:T(8,128)(2,1)}, bf16[512,1024]{1,0:T(8,128)(2,1)S(1)}, u32[]{:S(2)}, u32[]{:S(2)}) collective-permute-start(bf16[512,1024]{1,0:T(8,128)(2,1)} %get-tuple-element.90), channel_id=1, source_target_pairs={{1,2},{3,4},{5,6},{7,8},{9,10},{11,12},{13,14},{15,16},{17,18},{19... | collective-permute-start | bytes 3145736 | tf_op jit(solution)/shard_map/ppermute | solution.py:565
  15.6 40.9 %collective-permute-start.7 = (bf16[256,1024]{1,0:T(8,128)(2,1)}, bf16[256,1024]{1,0:T(8,128)(2,1)S(1)}, u32[]{:S(2)}, u32[]{:S(2)}) collective-permute-start(bf16[256,1024]{1,0:T(8,128)(2,1)} %get-tuple-element.107), channel_id=1, source_target_pairs={{1,2},{3,4},{5,6},{7,8},{9,10},{11,12},{13,14},{15,16},{17,18},{19... | collective-permute-start | bytes 1572872 | tf_op jit(solution)/shard_map/ppermute | solution.py:565
  20.6 31.2 %collective-permute-start.5 = (bf16[768,256]{1,0:T(8,128)(2,1)S(1)}, bf16[768,256]{1,0:T(8,128)(2,1)S(1)}, u32[]{:S(2)}, u32[]{:S(2)}) collective-permute-start(bf16[768,256]{1,0:T(8,128)(2,1)S(1)} %get-tuple-element.95), channel_id=1, source_target_pairs={{0,4},{4,8},{8,12},{12,16},{16,20},{20,24},{24,28},{1,5},{5,9},{9,... | collective-permute-start | bytes 1179656 | tf_op jit(solution)/shard_map/ppermute | solution.py:561
  23.8 28.0 %collective-permute-start.6 = (bf16[768,256]{1,0:T(8,128)(2,1)S(1)}, bf16[768,256]{1,0:T(8,128)(2,1)S(1)}, u32[]{:S(2)}, u32[]{:S(2)}) collective-permute-start(bf16[768,256]{1,0:T(8,128)(2,1)S(1)} %get-tuple-element.96), channel_id=1, source_target_pairs={{4,0},{8,4},{12,8},{16,12},{20,16},{24,20},{28,24},{5,1},{9,5},{13... | collective-permute-start | bytes 1179656 | tf_op jit(solution)/shard_map/ppermute | solution.py:561
  25.9 6.4 %collective-permute-start.3 = (bf16[768,1024]{1,0:T(8,128)(2,1)}, bf16[768,1024]{1,0:T(8,128)(2,1)S(1)}, u32[]{:S(2)}, u32[]{:S(2)}) collective-permute-start(bf16[768,1024]{1,0:T(8,128)(2,1)} %get-tuple-element.86), channel_id=1, source_target_pairs={{0,1},{2,3},{4,5},{6,7},{8,9},{10,11},{12,13},{14,15},{16,17},{18,... | collective-permute-start | bytes 4718600 | tf_op jit(solution)/shard_map/ppermute | solution.py:565
  54.2 6.2 %collective-permute-start.8 = (bf16[144,256]{1,0:T(8,128)(2,1)S(1)}, bf16[144,256]{1,0:T(8,128)(2,1)S(1)}, u32[]{:S(2)}, u32[]{:S(2)}) collective-permute-start(bf16[144,256]{1,0:T(8,128)(2,1)S(1)} %get-tuple-element.112), channel_id=1, source_target_pairs={{0,1},{1,0},{2,3},{3,2},{4,5},{5,4},{6,7},{7,6},{8,9},{9,8},{10,11... | collective-permute-start | bytes 221192 | tf_op jit(solution)/shard_map/ppermute | solution.py:588
  54.7 5.6 %collective-permute-start.9 = (bf16[144,256]{1,0:T(8,128)(2,1)S(1)}, bf16[144,256]{1,0:T(8,128)(2,1)S(1)}, u32[]{:S(2)}, u32[]{:S(2)}) collective-permute-start(bf16[144,256]{1,0:T(8,128)(2,1)S(1)} %get-tuple-element.113), channel_id=1, source_target_pairs={{0,2},{1,3},{2,0},{3,1},{4,6},{5,7},{6,4},{7,5},{8,10},{9,11},{10,... | collective-permute-start | bytes 221192 | tf_op jit(solution)/shard_map/ppermute | solution.py:588
  54.8 5.6 %collective-permute-start.10 = (bf16[144,256]{1,0:T(8,128)(2,1)S(1)}, bf16[144,256]{1,0:T(8,128)(2,1)S(1)}, u32[]{:S(2)}, u32[]{:S(2)}) collective-permute-start(bf16[144,256]{1,0:T(8,128)(2,1)S(1)} %get-tuple-element.114), channel_id=1, source_target_pairs={{0,3},{1,2},{2,1},{3,0},{4,7},{5,6},{6,5},{7,4},{8,11},{9,10},{10,... | collective-permute-start | bytes 221192 | tf_op jit(solution)/shard_map/ppermute | solution.py:588
where the time goes:
time: 63.6 us; the launch traced here: 63.4 us
  Pallas kernels  33.6 us (53%)
  starting transfers between devices  18.1 us (28%)
  waiting for transfers between devices  11.3 us (18%)
    pallas_call x6, Pallas kernels, run_shares(): pl.pallas_call(kernel, in_specs=[pl.BlockSpec(memory_space=pltpu.SMEM)] *...  26.4 us
    ppermute x3, starting transfers between devices, trade(): lax.ppermute(value, axis, pairs + [(target, source) for source, target in...  8.12 us
    ppermute x3, waiting for transfers between devices, trade(): lax.ppermute(value, axis, pairs + [(target, source) for source, target in...  5.79 us
    ppermute x2, starting transfers between devices, shift(): lax.ppermute(value, axis, [(source, source + steps) for source in range(f...  5.28 us
    ppermute x6, starting transfers between devices, exchange(): pieces[n] = lax.ppermute(pieces[n], 'grp', flips[n])  4.71 us
    ppermute x2, waiting for transfers between devices, shift(): lax.ppermute(value, axis, [(source, source + steps) for source in range(f...  4.12 us
    pallas_call x1, Pallas kernels, finish(): pl.pallas_call(finish_body, in_specs=[pl.BlockSpec(memory_space=pltpu.SME...  3.01 us
    pallas_call x1, Pallas kernels, coarse_levels(): pl.pallas_call(coarse_body, in_specs=[smem, smem, vmem, vmem, vmem], out_...  2.43 us
  transfers between devices with their start and end apart: 11, of which 3 were waited for; matrix products, arithmetic and copies ran while one was open for 0% of the time, Pallas kernels for 42%

commit v1 on v0

--- a/solution.py
+++ b/solution.py
@@ -594,14 +594,13 @@
     q0, q1, near, far, chip = rows_to_send(place, query_rows, key_vecs, value_vecs, groups)
     off_chip = [(device, device + 1) for device in range(1, count - 1, 2)]
     near = trade(near, everyone, off_chip)
-    far, pieces[1] = lax.optimization_barrier((far, pieces[1]))
-    far = trade(far, everyone, off_chip)
     pieces, chip = lax.optimization_barrier((pieces, chip))
     got, coarse_right, coarse_left = coarse_halos(place, pieces)
-    coarse_right, coarse_left, chip, q0 = lax.optimization_barrier((coarse_right, coarse_left, chip, q0))
+    coarse_right, coarse_left, chip, q0, far = lax.optimization_barrier((coarse_right, coarse_left, chip, q0, far))
     coarse_prev = shift(coarse_right, "seq", 1)
     coarse_next = shift(coarse_left, "seq", -1)
     chip = trade(chip, everyone, [(device, device + 1) for device in range(0, count - 1, 2)])
+    far = trade(far, everyone, off_chip)
     running = own_level(q0, key_vecs, value_vecs, groups)
     running = side_level(chip_body, "chip_level", place, bias, (q0, q1), running, chip)
     running = side_level(near_body, "near_level", place, bias, (q0, q1), running, near)

time: 63.6 us -> 63.6 us (level)
  no operation moved by 1% of the time
where the time goes in v1:
time: 63.6 us; the launch traced here: 63.4 us
  Pallas kernels  33.6 us (53%)
  starting transfers between devices  18.1 us (28%)
  waiting for transfers between devices  11.3 us (18%)
    pallas_call x6, Pallas kernels, run_shares(): pl.pallas_call(kernel, in_specs=[pl.BlockSpec(memory_space=pltpu.SMEM)] *...  26.4 us
    ppermute x3, starting transfers between devices, trade(): lax.ppermute(value, axis, pairs + [(target, source) for source, target in...  8.12 us
    ppermute x3, waiting for transfers between devices, trade(): lax.ppermute(value, axis, pairs + [(target, source) for source, target in...  5.83 us
    ppermute x2, starting transfers between devices, shift(): lax.ppermute(value, axis, [(source, source + steps) for source in range(f...  5.28 us
    ppermute x6, starting transfers between devices, exchange(): pieces[n] = lax.ppermute(pieces[n], 'grp', flips[n])  4.68 us
    ppermute x2, waiting for transfers between devices, shift(): lax.ppermute(value, axis, [(source, source + steps) for source in range(f...  4.13 us
    pallas_call x1, Pallas kernels, finish(): pl.pallas_call(finish_body, in_specs=[pl.BlockSpec(memory_space=pltpu.SME...  3 us
    pallas_call x1, Pallas kernels, coarse_levels(): pl.pallas_call(coarse_body, in_specs=[smem, smem, vmem, vmem, vmem], out_...  2.44 us
  transfers between devices with their start and end apart: 11, of which 3 were waited for; matrix products, arithmetic and copies ran while one was open for 0% of the time, Pallas kernels for 42%

profile of v1, /device:TPU:11, one launch (start us, length us, event | category | flops | bytes accessed | tf_op | source)
XLA Modules:
  0.0 63.4 jit_solution(13060506438962255516)
XLA Ops:
  0.1 3.9 %swap_rows.1 = (bf16[384,256]{1,0:T(8,128)(2,1)S(1)}, bf16[384,256]{1,0:T(8,128)(2,1)S(1)}, bf16[384,256]{1,0:T(8,128)(2,1)S(1)}, bf16[384,256]{1,0:T(8,128)(2,1)S(1)}) custom-call(s32[2]{0:T(128)S(1)} %pad_add_fusion.refs_0_.place_ref, bf16[512,1024]{1,0:T(8,128)(2,1)} %refs_1_.3, bf16[512,1024]{1,0:T(8,128)(2,1)} %refs_1_.4, bf16[512,1024]{1,0:T(8,128)(2,1)} %refs_2_.5), custom_call_target="tpu_custom_call" | custom-call | flops 1024 | bytes 1024 | tf_op jit(solution)/shard_map/swap_rows/pallas_call | solution.py:208
  4.0 0.7 %collective-permute-start = (bf16[384,256]{1,0:T(8,128)(2,1)S(1)}, bf16[384,256]{1,0:T(8,128)(2,1)S(1)}, u32[]{:S(2)}, u32[]{:S(2)}) collective-permute-start(bf16[384,256]{1,0:T(8,128)(2,1)S(1)} %get-tuple-element.66), channel_id=1, source_target_pairs={{0,1},{1,0},{2,3},{3,2},{4,5},{5,4},{6,7},{7,6},{8,9},{9,8},{10,11... | collective-permute-start | bytes 589832 | tf_op jit(solution)/shard_map/ppermute | solution.py:588
  4.8 1.3 %collective-permute-start.1 = (bf16[384,256]{1,0:T(8,128)(2,1)S(1)}, bf16[384,256]{1,0:T(8,128)(2,1)S(1)}, u32[]{:S(2)}, u32[]{:S(2)}) collective-permute-start(bf16[384,256]{1,0:T(8,128)(2,1)S(1)} %get-tuple-element.67), channel_id=1, source_target_pairs={{0,2},{1,3},{2,0},{3,1},{4,6},{5,7},{6,4},{7,5},{8,10},{9,11},{10,... | collective-permute-start | bytes 589832 | tf_op jit(solution)/shard_map/ppermute | solution.py:588
  6.0 0.5 collective-permute-start.2
  6.5 4.4 %rows_to_send.1 = (bf16[512,1024]{1,0:T(8,128)(2,1)}, bf16[256,1024]{1,0:T(8,128)(2,1)}, bf16[512,1024]{1,0:T(8,128)(2,1)}, bf16[256,1024]{1,0:T(8,128)(2,1)}, bf16[768,1024]{1,0:T(8,128)(2,1)}) custom-call(s32[2]{0:T(128)S(1)} %pad_add_fusion.refs_0_.place_ref, bf16[512,1024]{1,0:T(8,128)(2,1)} %refs_1_.3, bf16[512,1024]{1,0:T(8,128)(2,1)} %refs_1_.4, ...), custom_call_target="tpu_custom_call" | custom-call | flops 1024 | bytes 1024 | tf_op jit(solution)/shard_map/rows_to_send/pallas_call | solution.py:208
  10.8 3.2 %collective-permute-start.4 = (bf16[512,1024]{1,0:T(8,128)(2,1)}, bf16[512,1024]{1,0:T(8,128)(2,1)S(1)}, u32[]{:S(2)}, u32[]{:S(2)}) collective-permute-start(bf16[512,1024]{1,0:T(8,128)(2,1)} %get-tuple-element.88), channel_id=1, source_target_pairs={{1,2},{3,4},{5,6},{7,8},{9,10},{11,12},{13,14},{15,16},{17,18},{19... | collective-permute-start | bytes 3145736 | tf_op jit(solution)/shard_map/ppermute | solution.py:565
  14.1 0.1 add_select_fusion.refs_1_
  14.1 0.1 add_select_fusion.1.bias_ref
  14.2 1.4 %collective-permute-done.2.refs_3_ = bf16[384,256]{1,0:T(8,128)(2,1)S(1)} collective-permute-done((bf16[384,256]{1,0:T(8,128)(2,1)S(1)}, bf16[384,256]{1,0:T(8,128)(2,1)S(1)}, u32[]{:S(2)}, u32[]{:S(2)}) %collective-permute-start.2) | collective-permute-done | bytes 196640 | tf_op jit(solution)/shard_map/ppermute | solution.py:588
  15.6 1.7 %coarse_halos.1 = (bf16[4,384,256]{2,1,0:T(8,128)(2,1)S(1)}, bf16[768,256]{1,0:T(8,128)(2,1)S(1)}, bf16[768,256]{1,0:T(8,128)(2,1)S(1)}) custom-call(s32[2]{0:T(128)S(1)} %pad_add_fusion.refs_0_.place_ref, bf16[384,256]{1,0:T(8,128)(2,1)S(1)} %get-tuple-element.70.refs_0_, bf16[384,256]{1,0:T(8,128)(2,1)S(1)} %collective-permute-done.refs_1_, ...), custom_call_target="tpu_custom_call" | custom-call | flops 1048576 | bytes 2359296 | tf_op jit(solution)/shard_map/coarse_halos/pallas_call | solution.py:321
  17.3 3.2 %collective-permute-start.5 = (bf16[768,256]{1,0:T(8,128)(2,1)S(1)}, bf16[768,256]{1,0:T(8,128)(2,1)S(1)}, u32[]{:S(2)}, u32[]{:S(2)}) collective-permute-start(bf16[768,256]{1,0:T(8,128)(2,1)S(1)} %get-tuple-element.93), channel_id=1, source_target_pairs={{0,4},{4,8},{8,12},{12,16},{16,20},{20,24},{24,28},{1,5},{5,9},{9,... | collective-permute-start | bytes 1179656 | tf_op jit(solution)/shard_map/ppermute | solution.py:561
  20.5 2.1 %collective-permute-start.6 = (bf16[768,256]{1,0:T(8,128)(2,1)S(1)}, bf16[768,256]{1,0:T(8,128)(2,1)S(1)}, u32[]{:S(2)}, u32[]{:S(2)}) collective-permute-start(bf16[768,256]{1,0:T(8,128)(2,1)S(1)} %get-tuple-element.94), channel_id=1, source_target_pairs={{4,0},{8,4},{12,8},{16,12},{20,16},{24,20},{28,24},{5,1},{9,5},{13... | collective-permute-start | bytes 1179656 | tf_op jit(solution)/shard_map/ppermute | solution.py:561
  22.6 3.8 %collective-permute-start.7 = (bf16[256,1024]{1,0:T(8,128)(2,1)}, bf16[256,1024]{1,0:T(8,128)(2,1)S(1)}, u32[]{:S(2)}, u32[]{:S(2)}) collective-permute-start(bf16[256,1024]{1,0:T(8,128)(2,1)} %get-tuple-element.105), channel_id=1, source_target_pairs={{1,2},{3,4},{5,6},{7,8},{9,10},{11,12},{13,14},{15,16},{17,18},{19... | collective-permute-start | bytes 1572872 | tf_op jit(solution)/shard_map/ppermute | solution.py:565
  26.4 1.1 %collective-permute-start.3 = (bf16[768,1024]{1,0:T(8,128)(2,1)}, bf16[768,1024]{1,0:T(8,128)(2,1)S(1)}, u32[]{:S(2)}, u32[]{:S(2)}) collective-permute-start(bf16[768,1024]{1,0:T(8,128)(2,1)} %get-tuple-element.84), channel_id=1, source_target_pairs={{0,1},{2,3},{4,5},{6,7},{8,9},{10,11},{12,13},{14,15},{16,17},{18,... | collective-permute-start | bytes 4718600 | tf_op jit(solution)/shard_map/ppermute | solution.py:565
  27.5 4.7 %own_level.1 = (f32[4,512,256]{2,1,0:T(8,128)S(1)}, f32[4,512,256]{2,1,0:T(8,128)S(1)}, f32[4,512,256]{2,1,0:T(8,128)S(1)}) custom-call(bf16[512,1024]{1,0:T(8,128)(2,1)} %get-tuple-element.80.refs_0_.refs_2_, bf16[512,1024]{1,0:T(8,128)(2,1)} %refs_1_.4, bf16[512,1024]{1,0:T(8,128)(2,1)} %refs_2_.5), custom_call_target="tpu_custom_call" | custom-call | flops 68719476736 | bytes 1024 | tf_op jit(solution)/shard_map/own_level/pallas_call | solution.py:208
  32.3 5.0 %chip_level.1 = (f32[4,512,256]{2,1,0:T(8,128)S(1)}, f32[4,512,256]{2,1,0:T(8,128)S(1)}, f32[4,512,256]{2,1,0:T(8,128)S(1)}) custom-call(s32[2]{0:T(128)S(1)} %pad_add_fusion.refs_0_.place_ref, f32[2]{0:T(128)S(1)} %add_select_fusion.refs_1_, bf16[512,1024]{1,0:T(8,128)(2,1)} %get-tuple-element.80.refs_0_.refs_2_, ...), custom_call_target="tpu_custom_call" | custom-call | flops 1024 | bytes 1024 | tf_op jit(solution)/shard_map/chip_level/pallas_call | solution.py:208
  37.3 5.8 %collective-permute-done.4.refs_7_ = bf16[512,1024]{1,0:T(8,128)(2,1)S(1)} collective-permute-done((bf16[512,1024]{1,0:T(8,128)(2,1)}, bf16[512,1024]{1,0:T(8,128)(2,1)S(1)}, u32[]{:S(2)}, u32[]{:S(2)}) %collective-permute-start.4) | collective-permute-done | bytes 1048608 | tf_op jit(solution)/shard_map/ppermute | solution.py:565
  43.2 4.5 %near_level.1 = (f32[4,512,256]{2,1,0:T(8,128)S(1)}, f32[4,512,256]{2,1,0:T(8,128)S(1)}, f32[4,512,256]{2,1,0:T(8,128)S(1)}) custom-call(s32[2]{0:T(128)S(1)} %pad_add_fusion.refs_0_.place_ref, f32[2]{0:T(128)S(1)} %add_select_fusion.refs_1_, bf16[512,1024]{1,0:T(8,128)(2,1)} %get-tuple-element.80.refs_0_.refs_2_, ...), custom_call_target="tpu_custom_call" | custom-call | flops 1024 | bytes 1024 | tf_op jit(solution)/shard_map/near_level/pallas_call | solution.py:208
  47.6 4.1 %collective-permute-done.5.prev_ref = bf16[768,256]{1,0:T(8,128)(2,1)S(1)} collective-permute-done((bf16[768,256]{1,0:T(8,128)(2,1)S(1)}, bf16[768,256]{1,0:T(8,128)(2,1)S(1)}, u32[]{:S(2)}, u32[]{:S(2)}) %collective-permute-start.5) | collective-permute-done | bytes 393248 | tf_op jit(solution)/shard_map/ppermute | solution.py:561
  51.8 2.4 %coarse_levels.1 = (bf16[144,256]{1,0:T(8,128)(2,1)S(1)}, bf16[144,256]{1,0:T(8,128)(2,1)S(1)}, bf16[144,256]{1,0:T(8,128)(2,1)S(1)}, bf16[144,256]{1,0:T(8,128)(2,1)S(1)}) custom-call(s32[2]{0:T(128)S(1)} %pad_add_fusion.refs_0_.place_ref, f32[2]{0:T(128)S(1)} %add_select_fusion.1.bias_ref, bf16[4,384,256]{2,1,0:T(8,128)(2,1)S(1)} %get-tuple-element.92.got_ref, ...), custom_call_target="tpu_custom_call" | custom-call | flops 68719476736 | bytes 3145728 | tf_op jit(solution)/shard_map/coarse_levels/pallas_call | solution.py:429
  54.2 0.5 collective-permute-start.8
  54.8 1.7 %collective-permute-start.10 = (bf16[144,256]{1,0:T(8,128)(2,1)S(1)}, bf16[144,256]{1,0:T(8,128)(2,1)S(1)}, u32[]{:S(2)}, u32[]{:S(2)}) collective-permute-start(bf16[144,256]{1,0:T(8,128)(2,1)S(1)} %get-tuple-element.112), channel_id=1, source_target_pairs={{0,3},{1,2},{2,1},{3,0},{4,7},{5,6},{6,5},{7,4},{8,11},{9,10},{10,... | collective-permute-start | bytes 221192 | tf_op jit(solution)/shard_map/ppermute | solution.py:588
  56.5 3.9 %far_level.1 = (f32[4,512,256]{2,1,0:T(8,128)S(1)}, f32[4,512,256]{2,1,0:T(8,128)S(1)}, f32[4,512,256]{2,1,0:T(8,128)S(1)}) custom-call(s32[2]{0:T(128)S(1)} %pad_add_fusion.refs_0_.place_ref, f32[2]{0:T(128)S(1)} %add_select_fusion.refs_1_, bf16[256,1024]{1,0:T(8,128)(2,1)} %get-tuple-element.64.refs_3_.refs_2_, ...), custom_call_target="tpu_custom_call" | custom-call | flops 1024 | bytes 1024 | tf_op jit(solution)/shard_map/far_level/pallas_call | solution.py:208
  60.4 3.0 %finish.1 = bf16[512,1024]{1,0:T(8,128)(2,1)} custom-call(s32[2]{0:T(128)S(1)} %pad_add_fusion.refs_0_.place_ref, f32[4,512,256]{2,1,0:T(8,128)S(1)} %get-tuple-element.106.sum_ref, f32[4,512,256]{2,1,0:T(8,128)S(1)} %get-tuple-element.107.top_ref, f32[4,512,256]{2,1,0:T(8,128)S(1)} %get-tuple-element.108.total_ref, ...), custom_call_target="tpu_custom_call" | custom-call | flops 1024 | bytes 1024 | tf_op jit(solution)/shard_map/finish/pallas_call | solution.py:546
  (10 shorter events, 0.1 us)
Async XLA Ops:
  4.0 10.2 %collective-permute-start = (bf16[384,256]{1,0:T(8,128)(2,1)S(1)}, bf16[384,256]{1,0:T(8,128)(2,1)S(1)}, u32[]{:S(2)}, u32[]{:S(2)}) collective-permute-start(bf16[384,256]{1,0:T(8,128)(2,1)S(1)} %get-tuple-element.66), channel_id=1, source_target_pairs={{0,1},{1,0},{2,3},{3,2},{4,5},{5,4},{6,7},{7,6},{8,9},{9,8},{10,11... | collective-permute-start | bytes 589832 | tf_op jit(solution)/shard_map/ppermute | solution.py:588
  4.8 9.5 %collective-permute-start.1 = (bf16[384,256]{1,0:T(8,128)(2,1)S(1)}, bf16[384,256]{1,0:T(8,128)(2,1)S(1)}, u32[]{:S(2)}, u32[]{:S(2)}) collective-permute-start(bf16[384,256]{1,0:T(8,128)(2,1)S(1)} %get-tuple-element.67), channel_id=1, source_target_pairs={{0,2},{1,3},{2,0},{3,1},{4,6},{5,7},{6,4},{7,5},{8,10},{9,11},{10,... | collective-permute-start | bytes 589832 | tf_op jit(solution)/shard_map/ppermute | solution.py:588
  6.0 9.6 %collective-permute-start.2 = (bf16[384,256]{1,0:T(8,128)(2,1)S(1)}, bf16[384,256]{1,0:T(8,128)(2,1)S(1)}, u32[]{:S(2)}, u32[]{:S(2)}) collective-permute-start(bf16[384,256]{1,0:T(8,128)(2,1)S(1)} %get-tuple-element.68), channel_id=1, source_target_pairs={{0,3},{1,2},{2,1},{3,0},{4,7},{5,6},{6,5},{7,4},{8,11},{9,10},{10,... | collective-permute-start | bytes 589832 | tf_op jit(solution)/shard_map/ppermute | solution.py:588
  10.8 32.3 %collective-permute-start.4 = (bf16[512,1024]{1,0:T(8,128)(2,1)}, bf16[512,1024]{1,0:T(8,128)(2,1)S(1)}, u32[]{:S(2)}, u32[]{:S(2)}) collective-permute-start(bf16[512,1024]{1,0:T(8,128)(2,1)} %get-tuple-element.88), channel_id=1, source_target_pairs={{1,2},{3,4},{5,6},{7,8},{9,10},{11,12},{13,14},{15,16},{17,18},{19... | collective-permute-start | bytes 3145736 | tf_op jit(solution)/shard_map/ppermute | solution.py:565
  17.3 34.5 %collective-permute-start.5 = (bf16[768,256]{1,0:T(8,128)(2,1)S(1)}, bf16[768,256]{1,0:T(8,128)(2,1)S(1)}, u32[]{:S(2)}, u32[]{:S(2)}) collective-permute-start(bf16[768,256]{1,0:T(8,128)(2,1)S(1)} %get-tuple-element.93), channel_id=1, source_target_pairs={{0,4},{4,8},{8,12},{12,16},{16,20},{20,24},{24,28},{1,5},{5,9},{9,... | collective-permute-start | bytes 1179656 | tf_op jit(solution)/shard_map/ppermute | solution.py:561
  20.5 31.3 %collective-permute-start.6 = (bf16[768,256]{1,0:T(8,128)(2,1)S(1)}, bf16[768,256]{1,0:T(8,128)(2,1)S(1)}, u32[]{:S(2)}, u32[]{:S(2)}) collective-permute-start(bf16[768,256]{1,0:T(8,128)(2,1)S(1)} %get-tuple-element.94), channel_id=1, source_target_pairs={{4,0},{8,4},{12,8},{16,12},{20,16},{24,20},{28,24},{5,1},{9,5},{13... | collective-permute-start | bytes 1179656 | tf_op jit(solution)/shard_map/ppermute | solution.py:561
  22.6 33.9 %collective-permute-start.7 = (bf16[256,1024]{1,0:T(8,128)(2,1)}, bf16[256,1024]{1,0:T(8,128)(2,1)S(1)}, u32[]{:S(2)}, u32[]{:S(2)}) collective-permute-start(bf16[256,1024]{1,0:T(8,128)(2,1)} %get-tuple-element.105), channel_id=1, source_target_pairs={{1,2},{3,4},{5,6},{7,8},{9,10},{11,12},{13,14},{15,16},{17,18},{19... | collective-permute-start | bytes 1572872 | tf_op jit(solution)/shard_map/ppermute | solution.py:565
  26.4 5.8 %collective-permute-start.3 = (bf16[768,1024]{1,0:T(8,128)(2,1)}, bf16[768,1024]{1,0:T(8,128)(2,1)S(1)}, u32[]{:S(2)}, u32[]{:S(2)}) collective-permute-start(bf16[768,1024]{1,0:T(8,128)(2,1)} %get-tuple-element.84), channel_id=1, source_target_pairs={{0,1},{2,3},{4,5},{6,7},{8,9},{10,11},{12,13},{14,15},{16,17},{18,... | collective-permute-start | bytes 4718600 | tf_op jit(solution)/shard_map/ppermute | solution.py:565
  54.2 6.1 %collective-permute-start.8 = (bf16[144,256]{1,0:T(8,128)(2,1)S(1)}, bf16[144,256]{1,0:T(8,128)(2,1)S(1)}, u32[]{:S(2)}, u32[]{:S(2)}) collective-permute-start(bf16[144,256]{1,0:T(8,128)(2,1)S(1)} %get-tuple-element.110), channel_id=1, source_target_pairs={{0,1},{1,0},{2,3},{3,2},{4,5},{5,4},{6,7},{7,6},{8,9},{9,8},{10,11... | collective-permute-start | bytes 221192 | tf_op jit(solution)/shard_map/ppermute | solution.py:588
  54.7 5.6 %collective-permute-start.9 = (bf16[144,256]{1,0:T(8,128)(2,1)S(1)}, bf16[144,256]{1,0:T(8,128)(2,1)S(1)}, u32[]{:S(2)}, u32[]{:S(2)}) collective-permute-start(bf16[144,256]{1,0:T(8,128)(2,1)S(1)} %get-tuple-element.111), channel_id=1, source_target_pairs={{0,2},{1,3},{2,0},{3,1},{4,6},{5,7},{6,4},{7,5},{8,10},{9,11},{10,... | collective-permute-start | bytes 221192 | tf_op jit(solution)/shard_map/ppermute | solution.py:588
  54.8 5.6 %collective-permute-start.10 = (bf16[144,256]{1,0:T(8,128)(2,1)S(1)}, bf16[144,256]{1,0:T(8,128)(2,1)S(1)}, u32[]{:S(2)}, u32[]{:S(2)}) collective-permute-start(bf16[144,256]{1,0:T(8,128)(2,1)S(1)} %get-tuple-element.112), channel_id=1, source_target_pairs={{0,3},{1,2},{2,1},{3,0},{4,7},{5,6},{6,5},{7,4},{8,11},{9,10},{10,... | collective-permute-start | bytes 221192 | tf_op jit(solution)/shard_map/ppermute | solution.py:588

commit v2 on v1

--- a/solution.py
+++ b/solution.py
@@ -593,16 +593,22 @@
     pieces = exchange(pieces)
     q0, q1, near, far, chip = rows_to_send(place, query_rows, key_vecs, value_vecs, groups)
     off_chip = [(device, device + 1) for device in range(1, count - 1, 2)]
-    near = trade(near, everyone, off_chip)
+    near_out = trade(near, everyone, [pair for pair in off_chip if pair[1] % groups == 0])
     pieces, chip = lax.optimization_barrier((pieces, chip))
     got, coarse_right, coarse_left = coarse_halos(place, pieces)
-    coarse_right, coarse_left, chip, q0, far = lax.optimization_barrier((coarse_right, coarse_left, chip, q0, far))
+    coarse_right, coarse_left, chip, q0, far, near = lax.optimization_barrier(
+        (coarse_right, coarse_left, chip, q0, far, near)
+    )
     coarse_prev = shift(coarse_right, "seq", 1)
     coarse_next = shift(coarse_left, "seq", -1)
     chip = trade(chip, everyone, [(device, device + 1) for device in range(0, count - 1, 2)])
+    near_in = trade(near, everyone, [pair for pair in off_chip if pair[1] % groups != 0])
+    running = own_level(q0, key_vecs, value_vecs, groups)
+    far, running = lax.optimization_barrier((far, running))
     far = trade(far, everyone, off_chip)
-    running = own_level(q0, key_vecs, value_vecs, groups)
     running = side_level(chip_body, "chip_level", place, bias, (q0, q1), running, chip)
+    near_out, near_in, running = lax.optimization_barrier((near_out, near_in, running))
+    near = near_out + near_in
     running = side_level(near_body, "near_level", place, bias, (q0, q1), running, near)
     got, running = lax.optimization_barrier((got, running))
     back = coarse_levels(place, edge_bias("seq"), got, coarse_prev, coarse_next)

time: 63.6 us -> 63.7 us (level)
  starting transfers between devices: 18.1 us -> 17 us
    ppermute x2, waiting for transfers between devices: 4.13 us -> 1.54 us  [shift(): lax.ppermute(value, axis, [(source, source + steps) for source in range(f...]
    ppermute x6, waiting for transfers between devices: 1.39 us -> 3.86 us  [exchange(): pieces[n] = lax.ppermute(pieces[n], 'grp', flips[n])]
    ppermute x3 -> x4, starting transfers between devices: 8.12 us -> 7.14 us  [trade(): lax.ppermute(value, axis, pairs + [(target, source) for source, target in...]
    ppermute x3 -> x4, waiting for transfers between devices: 5.83 us -> 6.38 us  [trade(): lax.ppermute(value, axis, pairs + [(target, source) for source, target in...]
  transfers between devices with their start and end apart: 11 -> 12, of which waited for: 3 -> 3; matrix products, arithmetic and copies ran while one was open for 0% -> 1% of each run, Pallas kernels for 42% -> 42%
where the time goes in v2:
time: 63.7 us; the launch traced here: 63.1 us
  Pallas kernels  33.6 us (53%)
  starting transfers between devices  17 us (27%)
  waiting for transfers between devices  11.8 us (19%)
    pallas_call x6, Pallas kernels, run_shares(): pl.pallas_call(kernel, in_specs=[pl.BlockSpec(memory_space=pltpu.SMEM)] *...  26.4 us
    ppermute x4, starting transfers between devices, trade(): lax.ppermute(value, axis, pairs + [(target, source) for source, target in...  7.14 us
    ppermute x4, waiting for transfers between devices, trade(): lax.ppermute(value, axis, pairs + [(target, source) for source, target in...  6.38 us
    ppermute x2, starting transfers between devices, shift(): lax.ppermute(value, axis, [(source, source + steps) for source in range(f...  5.28 us
    ppermute x6, starting transfers between devices, exchange(): pieces[n] = lax.ppermute(pieces[n], 'grp', flips[n])  4.54 us
    ppermute x6, waiting for transfers between devices, exchange(): pieces[n] = lax.ppermute(pieces[n], 'grp', flips[n])  3.86 us
    pallas_call x1, Pallas kernels, finish(): pl.pallas_call(finish_body, in_specs=[pl.BlockSpec(memory_space=pltpu.SME...  3 us
    pallas_call x1, Pallas kernels, coarse_levels(): pl.pallas_call(coarse_body, in_specs=[smem, smem, vmem, vmem, vmem], out_...  2.43 us
  transfers between devices with their start and end apart: 12, of which 3 were waited for; matrix products, arithmetic and copies ran while one was open for 1% of the time, Pallas kernels for 42%

profile of v2, /device:TPU:11, one launch (start us, length us, event | category | flops | bytes accessed | tf_op | source)
XLA Modules:
  0.0 63.1 jit_solution(5970567292298809075)
XLA Ops:
  0.1 3.9 %swap_rows.1 = (bf16[384,256]{1,0:T(8,128)(2,1)S(1)}, bf16[384,256]{1,0:T(8,128)(2,1)S(1)}, bf16[384,256]{1,0:T(8,128)(2,1)S(1)}, bf16[384,256]{1,0:T(8,128)(2,1)S(1)}) custom-call(s32[2]{0:T(128)S(1)} %pad_add_fusion.refs_0_.place_ref, bf16[512,1024]{1,0:T(8,128)(2,1)} %refs_1_.3, bf16[512,1024]{1,0:T(8,128)(2,1)} %refs_1_.4, bf16[512,1024]{1,0:T(8,128)(2,1)} %refs_2_.5), custom_call_target="tpu_custom_call" | custom-call | flops 1024 | bytes 1024 | tf_op jit(solution)/shard_map/swap_rows/pallas_call | solution.py:208
  4.0 0.7 %collective-permute-start = (bf16[384,256]{1,0:T(8,128)(2,1)S(1)}, bf16[384,256]{1,0:T(8,128)(2,1)S(1)}, u32[]{:S(2)}, u32[]{:S(2)}) collective-permute-start(bf16[384,256]{1,0:T(8,128)(2,1)S(1)} %get-tuple-element.76), channel_id=1, source_target_pairs={{0,1},{1,0},{2,3},{3,2},{4,5},{5,4},{6,7},{7,6},{8,9},{9,8},{10,11... | collective-permute-start | bytes 589832 | tf_op jit(solution)/shard_map/ppermute | solution.py:588
  4.8 1.3 %collective-permute-start.1 = (bf16[384,256]{1,0:T(8,128)(2,1)S(1)}, bf16[384,256]{1,0:T(8,128)(2,1)S(1)}, u32[]{:S(2)}, u32[]{:S(2)}) collective-permute-start(bf16[384,256]{1,0:T(8,128)(2,1)S(1)} %get-tuple-element.77), channel_id=1, source_target_pairs={{0,2},{1,3},{2,0},{3,1},{4,6},{5,7},{6,4},{7,5},{8,10},{9,11},{10,... | collective-permute-start | bytes 589832 | tf_op jit(solution)/shard_map/ppermute | solution.py:588
  6.0 0.5 collective-permute-start.2
  6.5 4.4 %rows_to_send.1 = (bf16[512,1024]{1,0:T(8,128)(2,1)}, bf16[256,1024]{1,0:T(8,128)(2,1)}, bf16[512,1024]{1,0:T(8,128)(2,1)}, bf16[256,1024]{1,0:T(8,128)(2,1)}, bf16[768,1024]{1,0:T(8,128)(2,1)}) custom-call(s32[2]{0:T(128)S(1)} %pad_add_fusion.refs_0_.place_ref, bf16[512,1024]{1,0:T(8,128)(2,1)} %refs_1_.3, bf16[512,1024]{1,0:T(8,128)(2,1)} %refs_1_.4, ...), custom_call_target="tpu_custom_call" | custom-call | flops 1024 | bytes 1024 | tf_op jit(solution)/shard_map/rows_to_send/pallas_call | solution.py:208
  10.8 0.7 %collective-permute-start.3 = (bf16[512,1024]{1,0:T(8,128)(2,1)}, bf16[512,1024]{1,0:T(8,128)(2,1)S(1)}, u32[]{:S(2)}, u32[]{:S(2)}) collective-permute-start(bf16[512,1024]{1,0:T(8,128)(2,1)} %get-tuple-element.92), channel_id=1, source_target_pairs={{3,4},{7,8},{11,12},{15,16},{19,20},{23,24},{27,28},{4,3},{8,7},{1... | collective-permute-start | bytes 3145736 | tf_op jit(solution)/shard_map/ppermute | solution.py:565
  11.6 0.1 add_select_fusion.refs_1_
  11.8 3.9 %collective-permute-done.2.refs_3_ = bf16[384,256]{1,0:T(8,128)(2,1)S(1)} collective-permute-done((bf16[384,256]{1,0:T(8,128)(2,1)S(1)}, bf16[384,256]{1,0:T(8,128)(2,1)S(1)}, u32[]{:S(2)}, u32[]{:S(2)}) %collective-permute-start.2) | collective-permute-done | bytes 196640 | tf_op jit(solution)/shard_map/ppermute | solution.py:588
  15.6 1.7 %coarse_halos.1 = (bf16[4,384,256]{2,1,0:T(8,128)(2,1)S(1)}, bf16[768,256]{1,0:T(8,128)(2,1)S(1)}, bf16[768,256]{1,0:T(8,128)(2,1)S(1)}) custom-call(s32[2]{0:T(128)S(1)} %pad_add_fusion.refs_0_.place_ref, bf16[384,256]{1,0:T(8,128)(2,1)S(1)} %get-tuple-element.80.refs_0_, bf16[384,256]{1,0:T(8,128)(2,1)S(1)} %collective-permute-done.refs_1_, ...), custom_call_target="tpu_custom_call" | custom-call | flops 1048576 | bytes 2359296 | tf_op jit(solution)/shard_map/coarse_halos/pallas_call | solution.py:321
  17.3 0.3 collective-permute-start.5
  17.6 3.3 %collective-permute-start.4 = (bf16[512,1024]{1,0:T(8,128)(2,1)}, bf16[512,1024]{1,0:T(8,128)(2,1)S(1)}, u32[]{:S(2)}, u32[]{:S(2)}) collective-permute-start(bf16[512,1024]{1,0:T(8,128)(2,1)} %get-tuple-element.92), channel_id=1, source_target_pairs={{1,2},{5,6},{9,10},{13,14},{17,18},{21,22},{25,26},{29,30},{2,1},{... | collective-permute-start | bytes 3145736 | tf_op jit(solution)/shard_map/ppermute | solution.py:565
  20.9 3.2 %collective-permute-start.6 = (bf16[768,256]{1,0:T(8,128)(2,1)S(1)}, bf16[768,256]{1,0:T(8,128)(2,1)S(1)}, u32[]{:S(2)}, u32[]{:S(2)}) collective-permute-start(bf16[768,256]{1,0:T(8,128)(2,1)S(1)} %get-tuple-element.113), channel_id=1, source_target_pairs={{0,4},{4,8},{8,12},{12,16},{16,20},{20,24},{24,28},{1,5},{5,9},{9,... | collective-permute-start | bytes 1179656 | tf_op jit(solution)/shard_map/ppermute | solution.py:561
  24.1 2.1 %collective-permute-start.7 = (bf16[768,256]{1,0:T(8,128)(2,1)S(1)}, bf16[768,256]{1,0:T(8,128)(2,1)S(1)}, u32[]{:S(2)}, u32[]{:S(2)}) collective-permute-start(bf16[768,256]{1,0:T(8,128)(2,1)S(1)} %get-tuple-element.114), channel_id=1, source_target_pairs={{4,0},{8,4},{12,8},{16,12},{20,16},{24,20},{28,24},{5,1},{9,5},{13... | collective-permute-start | bytes 1179656 | tf_op jit(solution)/shard_map/ppermute | solution.py:561
  26.2 4.8 %own_level.1 = (f32[4,512,256]{2,1,0:T(8,128)S(1)}, f32[4,512,256]{2,1,0:T(8,128)S(1)}, f32[4,512,256]{2,1,0:T(8,128)S(1)}) custom-call(bf16[512,1024]{1,0:T(8,128)(2,1)} %get-tuple-element.91.refs_0_.refs_2_, bf16[512,1024]{1,0:T(8,128)(2,1)} %refs_1_.4, bf16[512,1024]{1,0:T(8,128)(2,1)} %refs_2_.5), custom_call_target="tpu_custom_call" | custom-call | flops 68719476736 | bytes 1024 | tf_op jit(solution)/shard_map/own_level/pallas_call | solution.py:208
  31.0 2.8 %collective-permute-start.8 = (bf16[256,1024]{1,0:T(8,128)(2,1)S(1)}, bf16[256,1024]{1,0:T(8,128)(2,1)S(1)}, u32[]{:S(2)}, u32[]{:S(2)}) collective-permute-start(bf16[256,1024]{1,0:T(8,128)(2,1)S(1)} %copy-done), channel_id=1, source_target_pairs={{1,2},{3,4},{5,6},{7,8},{9,10},{11,12},{13,14},{15,16},{17,18},{19... | collective-permute-start | bytes 1572872 | tf_op jit(solution)/shard_map/ppermute | solution.py:565
  33.8 5.0 %chip_level.1 = (f32[4,512,256]{2,1,0:T(8,128)S(1)}, f32[4,512,256]{2,1,0:T(8,128)S(1)}, f32[4,512,256]{2,1,0:T(8,128)S(1)}) custom-call(s32[2]{0:T(128)S(1)} %pad_add_fusion.refs_0_.place_ref, f32[2]{0:T(128)S(1)} %add_select_fusion.refs_1_, bf16[512,1024]{1,0:T(8,128)(2,1)} %get-tuple-element.91.refs_0_.refs_2_, ...), custom_call_target="tpu_custom_call" | custom-call | flops 1024 | bytes 1024 | tf_op jit(solution)/shard_map/chip_level/pallas_call | solution.py:208
  38.9 6.4 %collective-permute-done.4 = bf16[512,1024]{1,0:T(8,128)(2,1)S(1)} collective-permute-done((bf16[512,1024]{1,0:T(8,128)(2,1)}, bf16[512,1024]{1,0:T(8,128)(2,1)S(1)}, u32[]{:S(2)}, u32[]{:S(2)}) %collective-permute-start.4) | collective-permute-done | bytes 1048608 | tf_op jit(solution)/shard_map/ppermute | solution.py:565
  45.3 0.4 add.7.refs_7_
  45.7 4.5 %near_level.1 = (f32[4,512,256]{2,1,0:T(8,128)S(1)}, f32[4,512,256]{2,1,0:T(8,128)S(1)}, f32[4,512,256]{2,1,0:T(8,128)S(1)}) custom-call(s32[2]{0:T(128)S(1)} %pad_add_fusion.refs_0_.place_ref, f32[2]{0:T(128)S(1)} %add_select_fusion.refs_1_, bf16[512,1024]{1,0:T(8,128)(2,1)} %get-tuple-element.91.refs_0_.refs_2_, ...), custom_call_target="tpu_custom_call" | custom-call | flops 1024 | bytes 1024 | tf_op jit(solution)/shard_map/near_level/pallas_call | solution.py:208
  50.2 1.5 %collective-permute-done.6.prev_ref = bf16[768,256]{1,0:T(8,128)(2,1)S(1)} collective-permute-done((bf16[768,256]{1,0:T(8,128)(2,1)S(1)}, bf16[768,256]{1,0:T(8,128)(2,1)S(1)}, u32[]{:S(2)}, u32[]{:S(2)}) %collective-permute-start.6) | collective-permute-done | bytes 393248 | tf_op jit(solution)/shard_map/ppermute | solution.py:561
  51.7 2.4 %coarse_levels.1 = (bf16[144,256]{1,0:T(8,128)(2,1)S(1)}, bf16[144,256]{1,0:T(8,128)(2,1)S(1)}, bf16[144,256]{1,0:T(8,128)(2,1)S(1)}, bf16[144,256]{1,0:T(8,128)(2,1)S(1)}) custom-call(s32[2]{0:T(128)S(1)} %pad_add_fusion.refs_0_.place_ref, f32[2]{0:T(128)S(1)} %add_select_fusion.1.bias_ref, bf16[4,384,256]{2,1,0:T(8,128)(2,1)S(1)} %get-tuple-element.112.got_ref, ...), custom_call_target="tpu_custom_call" | custom-call | flops 68719476736 | bytes 3145728 | tf_op jit(solution)/shard_map/coarse_levels/pallas_call | solution.py:429
  54.2 2.0 %collective-permute-start.11 = (bf16[144,256]{1,0:T(8,128)(2,1)S(1)}, bf16[144,256]{1,0:T(8,128)(2,1)S(1)}, u32[]{:S(2)}, u32[]{:S(2)}) collective-permute-start(bf16[144,256]{1,0:T(8,128)(2,1)S(1)} %get-tuple-element.132), channel_id=1, source_target_pairs={{0,3},{1,2},{2,1},{3,0},{4,7},{5,6},{6,5},{7,4},{8,11},{9,10},{10,... | collective-permute-start | bytes 221192 | tf_op jit(solution)/shard_map/ppermute | solution.py:588
  56.2 3.9 %far_level.1 = (f32[4,512,256]{2,1,0:T(8,128)S(1)}, f32[4,512,256]{2,1,0:T(8,128)S(1)}, f32[4,512,256]{2,1,0:T(8,128)S(1)}) custom-call(s32[2]{0:T(128)S(1)} %pad_add_fusion.refs_0_.place_ref, f32[2]{0:T(128)S(1)} %add_select_fusion.refs_1_, bf16[256,1024]{1,0:T(8,128)(2,1)} %get-tuple-element.74.refs_3_.refs_2_, ...), custom_call_target="tpu_custom_call" | custom-call | flops 1024 | bytes 1024 | tf_op jit(solution)/shard_map/far_level/pallas_call | solution.py:208
  60.1 3.0 %finish.1 = bf16[512,1024]{1,0:T(8,128)(2,1)} custom-call(s32[2]{0:T(128)S(1)} %pad_add_fusion.refs_0_.place_ref, f32[4,512,256]{2,1,0:T(8,128)S(1)} %get-tuple-element.126.sum_ref, f32[4,512,256]{2,1,0:T(8,128)S(1)} %get-tuple-element.127.top_ref, f32[4,512,256]{2,1,0:T(8,128)S(1)} %get-tuple-element.128.total_ref, ...), custom_call_target="tpu_custom_call" | custom-call | flops 1024 | bytes 1024 | tf_op jit(solution)/shard_map/finish/pallas_call | solution.py:546
  (15 shorter events, 0.3 us)
Async XLA Ops:
  4.0 7.7 %collective-permute-start = (bf16[384,256]{1,0:T(8,128)(2,1)S(1)}, bf16[384,256]{1,0:T(8,128)(2,1)S(1)}, u32[]{:S(2)}, u32[]{:S(2)}) collective-permute-start(bf16[384,256]{1,0:T(8,128)(2,1)S(1)} %get-tuple-element.76), channel_id=1, source_target_pairs={{0,1},{1,0},{2,3},{3,2},{4,5},{5,4},{6,7},{7,6},{8,9},{9,8},{10,11... | collective-permute-start | bytes 589832 | tf_op jit(solution)/shard_map/ppermute | solution.py:588
  4.8 7.0 %collective-permute-start.1 = (bf16[384,256]{1,0:T(8,128)(2,1)S(1)}, bf16[384,256]{1,0:T(8,128)(2,1)S(1)}, u32[]{:S(2)}, u32[]{:S(2)}) collective-permute-start(bf16[384,256]{1,0:T(8,128)(2,1)S(1)} %get-tuple-element.77), channel_id=1, source_target_pairs={{0,2},{1,3},{2,0},{3,1},{4,6},{5,7},{6,4},{7,5},{8,10},{9,11},{10,... | collective-permute-start | bytes 589832 | tf_op jit(solution)/shard_map/ppermute | solution.py:588
  6.0 9.6 %collective-permute-start.2 = (bf16[384,256]{1,0:T(8,128)(2,1)S(1)}, bf16[384,256]{1,0:T(8,128)(2,1)S(1)}, u32[]{:S(2)}, u32[]{:S(2)}) collective-permute-start(bf16[384,256]{1,0:T(8,128)(2,1)S(1)} %get-tuple-element.78), channel_id=1, source_target_pairs={{0,3},{1,2},{2,1},{3,0},{4,7},{5,6},{6,5},{7,4},{8,11},{9,10},{10,... | collective-permute-start | bytes 589832 | tf_op jit(solution)/shard_map/ppermute | solution.py:588
  10.8 28.0 %collective-permute-start.3 = (bf16[512,1024]{1,0:T(8,128)(2,1)}, bf16[512,1024]{1,0:T(8,128)(2,1)S(1)}, u32[]{:S(2)}, u32[]{:S(2)}) collective-permute-start(bf16[512,1024]{1,0:T(8,128)(2,1)} %get-tuple-element.92), channel_id=1, source_target_pairs={{3,4},{7,8},{11,12},{15,16},{19,20},{23,24},{27,28},{4,3},{8,7},{1... | collective-permute-start | bytes 3145736 | tf_op jit(solution)/shard_map/ppermute | solution.py:565
  17.3 13.7 %copy-start = (bf16[256,1024]{1,0:T(8,128)(2,1)S(1)}, bf16[256,1024]{1,0:T(8,128)(2,1)}, u32[]{:S(2)}) copy-start(bf16[256,1024]{1,0:T(8,128)(2,1)} %get-tuple-element.125) | copy-start | bytes 1572868
  17.3 13.7 %collective-permute-start.5 = (bf16[768,1024]{1,0:T(8,128)(2,1)}, bf16[768,1024]{1,0:T(8,128)(2,1)S(1)}, u32[]{:S(2)}, u32[]{:S(2)}) collective-permute-start(bf16[768,1024]{1,0:T(8,128)(2,1)} %get-tuple-element.100), channel_id=1, source_target_pairs={{0,1},{2,3},{4,5},{6,7},{8,9},{10,11},{12,13},{14,15},{16,17},{18,... | collective-permute-start | bytes 4718600 | tf_op jit(solution)/shard_map/ppermute | solution.py:565
  17.6 27.6 %collective-permute-start.4 = (bf16[512,1024]{1,0:T(8,128)(2,1)}, bf16[512,1024]{1,0:T(8,128)(2,1)S(1)}, u32[]{:S(2)}, u32[]{:S(2)}) collective-permute-start(bf16[512,1024]{1,0:T(8,128)(2,1)} %get-tuple-element.92), channel_id=1, source_target_pairs={{1,2},{5,6},{9,10},{13,14},{17,18},{21,22},{25,26},{29,30},{2,1},{... | collective-permute-start | bytes 3145736 | tf_op jit(solution)/shard_map/ppermute | solution.py:565
  20.9 30.8 %collective-permute-start.6 = (bf16[768,256]{1,0:T(8,128)(2,1)S(1)}, bf16[768,256]{1,0:T(8,128)(2,1)S(1)}, u32[]{:S(2)}, u32[]{:S(2)}) collective-permute-start(bf16[768,256]{1,0:T(8,128)(2,1)S(1)} %get-tuple-element.113), channel_id=1, source_target_pairs={{0,4},{4,8},{8,12},{12,16},{16,20},{20,24},{24,28},{1,5},{5,9},{9,... | collective-permute-start | bytes 1179656 | tf_op jit(solution)/shard_map/ppermute | solution.py:561
  24.1 27.6 %collective-permute-start.7 = (bf16[768,256]{1,0:T(8,128)(2,1)S(1)}, bf16[768,256]{1,0:T(8,128)(2,1)S(1)}, u32[]{:S(2)}, u32[]{:S(2)}) collective-permute-start(bf16[768,256]{1,0:T(8,128)(2,1)S(1)} %get-tuple-element.114), channel_id=1, source_target_pairs={{4,0},{8,4},{12,8},{16,12},{20,16},{24,20},{28,24},{5,1},{9,5},{13... | collective-permute-start | bytes 1179656 | tf_op jit(solution)/shard_map/ppermute | solution.py:561
  31.0 25.2 %collective-permute-start.8 = (bf16[256,1024]{1,0:T(8,128)(2,1)S(1)}, bf16[256,1024]{1,0:T(8,128)(2,1)S(1)}, u32[]{:S(2)}, u32[]{:S(2)}) collective-permute-start(bf16[256,1024]{1,0:T(8,128)(2,1)S(1)} %copy-done), channel_id=1, source_target_pairs={{1,2},{3,4},{5,6},{7,8},{9,10},{11,12},{13,14},{15,16},{17,18},{19... | collective-permute-start | bytes 1572872 | tf_op jit(solution)/shard_map/ppermute | solution.py:565
  54.1 6.0 %collective-permute-start.10 = (bf16[144,256]{1,0:T(8,128)(2,1)S(1)}, bf16[144,256]{1,0:T(8,128)(2,1)S(1)}, u32[]{:S(2)}, u32[]{:S(2)}) collective-permute-start(bf16[144,256]{1,0:T(8,128)(2,1)S(1)} %get-tuple-element.131), channel_id=1, source_target_pairs={{0,2},{1,3},{2,0},{3,1},{4,6},{5,7},{6,4},{7,5},{8,10},{9,11},{10,... | collective-permute-start | bytes 221192 | tf_op jit(solution)/shard_map/ppermute | solution.py:588
  54.2 5.9 %collective-permute-start.11 = (bf16[144,256]{1,0:T(8,128)(2,1)S(1)}, bf16[144,256]{1,0:T(8,128)(2,1)S(1)}, u32[]{:S(2)}, u32[]{:S(2)}) collective-permute-start(bf16[144,256]{1,0:T(8,128)(2,1)S(1)} %get-tuple-element.132), channel_id=1, source_target_pairs={{0,3},{1,2},{2,1},{3,0},{4,7},{5,6},{6,5},{7,4},{8,11},{9,10},{10,... | collective-permute-start | bytes 221192 | tf_op jit(solution)/shard_map/ppermute | solution.py:588
  56.2 3.9 %collective-permute-start.9 = (bf16[144,256]{1,0:T(8,128)(2,1)S(1)}, bf16[144,256]{1,0:T(8,128)(2,1)S(1)}, u32[]{:S(2)}, u32[]{:S(2)}) collective-permute-start(bf16[144,256]{1,0:T(8,128)(2,1)S(1)} %get-tuple-element.130), channel_id=1, source_target_pairs={{0,1},{1,0},{2,3},{3,2},{4,5},{5,4},{6,7},{7,6},{8,9},{9,8},{10,11... | collective-permute-start | bytes 221192 | tf_op jit(solution)/shard_map/ppermute | solution.py:588

commit v3 on v1

--- a/solution.py
+++ b/solution.py
@@ -582,16 +582,19 @@
     place = jnp.stack([odd, spot]).astype(jnp.int32)
     bias = edge_bias(everyone)
 
-    def exchange(pieces):
-        flips = [[(source, source ^ n) for source in range(groups)] for n in range(groups)]
-        for n in range(groups - 1, 0, -1):
-            pieces[n] = lax.ppermute(pieces[n], "grp", flips[n])
+    def exchange(pieces, places):
+        for n in places:
+            flips = [(source, source ^ n) for source in range(groups)]
+            pieces[n] = lax.ppermute(pieces[n], "grp", flips)
         return pieces
 
+    off = range(2, groups)
     pieces = list(swap_rows(place, query_vecs, key_vecs, value_vecs, groups))
     query_rows, pieces = lax.optimization_barrier((query_vecs, pieces))
-    pieces = exchange(pieces)
+    pieces = exchange(pieces, off)
     q0, q1, near, far, chip = rows_to_send(place, query_rows, key_vecs, value_vecs, groups)
+    pieces[1], far = lax.optimization_barrier((pieces[1], far))
+    pieces = exchange(pieces, [1])
     off_chip = [(device, device + 1) for device in range(1, count - 1, 2)]
     near = trade(near, everyone, off_chip)
     pieces, chip = lax.optimization_barrier((pieces, chip))
@@ -607,7 +610,7 @@
     got, running = lax.optimization_barrier((got, running))
     back = coarse_levels(place, edge_bias("seq"), got, coarse_prev, coarse_next)
     back, running = lax.optimization_barrier((back, running))
-    back = exchange(list(back))
+    back = exchange(list(back), [*off, 1])
     running = side_level(far_body, "far_level", place, bias, (q1,), running, far)
     return finish(place, running, back)
 

time: 63.6 us -> 63.7 us (level)
    ppermute x3, waiting for transfers between devices: 5.83 us -> 7.07 us  [trade(): lax.ppermute(value, axis, pairs + [(target, source) for source, target in...]
    ppermute x6, waiting for transfers between devices: 1.39 us -> 0.39 us  [exchange(): pieces[n] = lax.ppermute(pieces[n], 'grp', flips)]
where the time goes in v3:
time: 63.7 us; the launch traced here: 63.4 us
  Pallas kernels  33.6 us (53%)
  starting transfers between devices  17.9 us (28%)
  waiting for transfers between devices  11.5 us (18%)
    pallas_call x6, Pallas kernels, run_shares(): pl.pallas_call(kernel, in_specs=[pl.BlockSpec(memory_space=pltpu.SMEM)] *...  26.4 us
    ppermute x3, starting transfers between devices, trade(): lax.ppermute(value, axis, pairs + [(target, source) for source, target in...  8 us
    ppermute x3, waiting for transfers between devices, trade(): lax.ppermute(value, axis, pairs + [(target, source) for source, target in...  7.07 us
    ppermute x2, starting transfers between devices, shift(): lax.ppermute(value, axis, [(source, source + steps) for source in range(f...  5.28 us
    ppermute x6, starting transfers between devices, exchange(): pieces[n] = lax.ppermute(pieces[n], 'grp', flips)  4.64 us
    ppermute x2, waiting for transfers between devices, shift(): lax.ppermute(value, axis, [(source, source + steps) for source in range(f...  4.04 us
    pallas_call x1, Pallas kernels, finish(): pl.pallas_call(finish_body, in_specs=[pl.BlockSpec(memory_space=pltpu.SME...  3 us
    pallas_call x1, Pallas kernels, coarse_levels(): pl.pallas_call(coarse_body, in_specs=[smem, smem, vmem, vmem, vmem], out_...  2.43 us
  transfers between devices with their start and end apart: 11, of which 3 were waited for; matrix products, arithmetic and copies ran while one was open for 0% of the time, Pallas kernels for 42%

profile of v3, /device:TPU:11, one launch (start us, length us, event | category | flops | bytes accessed | tf_op | source)
XLA Modules:
  0.0 63.4 jit_solution(10699879704295714064)
XLA Ops:
  0.0 0.1 pad_add_fusion.refs_0_.place_ref
  0.1 3.9 %swap_rows.1 = (bf16[384,256]{1,0:T(8,128)(2,1)S(1)}, bf16[384,256]{1,0:T(8,128)(2,1)S(1)}, bf16[384,256]{1,0:T(8,128)(2,1)S(1)}, bf16[384,256]{1,0:T(8,128)(2,1)S(1)}) custom-call(s32[2]{0:T(128)S(1)} %pad_add_fusion.refs_0_.place_ref, bf16[512,1024]{1,0:T(8,128)(2,1)} %refs_1_.3, bf16[512,1024]{1,0:T(8,128)(2,1)} %refs_1_.4, bf16[512,1024]{1,0:T(8,128)(2,1)} %refs_2_.5), custom_call_target="tpu_custom_call" | custom-call | flops 1024 | bytes 1024 | tf_op jit(solution)/shard_map/swap_rows/pallas_call | solution.py:208
  4.0 1.3 %collective-permute-start.1 = (bf16[384,256]{1,0:T(8,128)(2,1)S(1)}, bf16[384,256]{1,0:T(8,128)(2,1)S(1)}, u32[]{:S(2)}, u32[]{:S(2)}) collective-permute-start(bf16[384,256]{1,0:T(8,128)(2,1)S(1)} %get-tuple-element.71), channel_id=1, source_target_pairs={{0,2},{1,3},{2,0},{3,1},{4,6},{5,7},{6,4},{7,5},{8,10},{9,11},{10,... | collective-permute-start | bytes 589832 | tf_op jit(solution)/shard_map/ppermute | solution.py:588
  5.3 1.1 %collective-permute-start.2 = (bf16[384,256]{1,0:T(8,128)(2,1)S(1)}, bf16[384,256]{1,0:T(8,128)(2,1)S(1)}, u32[]{:S(2)}, u32[]{:S(2)}) collective-permute-start(bf16[384,256]{1,0:T(8,128)(2,1)S(1)} %get-tuple-element.72), channel_id=1, source_target_pairs={{0,3},{1,2},{2,1},{3,0},{4,7},{5,6},{6,5},{7,4},{8,11},{9,10},{10,... | collective-permute-start | bytes 589832 | tf_op jit(solution)/shard_map/ppermute | solution.py:588
  6.4 4.4 %rows_to_send.1 = (bf16[512,1024]{1,0:T(8,128)(2,1)}, bf16[256,1024]{1,0:T(8,128)(2,1)}, bf16[512,1024]{1,0:T(8,128)(2,1)}, bf16[256,1024]{1,0:T(8,128)(2,1)}, bf16[768,1024]{1,0:T(8,128)(2,1)}) custom-call(s32[2]{0:T(128)S(1)} %pad_add_fusion.refs_0_.place_ref, bf16[512,1024]{1,0:T(8,128)(2,1)} %refs_1_.3, bf16[512,1024]{1,0:T(8,128)(2,1)} %refs_1_.4, ...), custom_call_target="tpu_custom_call" | custom-call | flops 1024 | bytes 1024 | tf_op jit(solution)/shard_map/rows_to_send/pallas_call | solution.py:208
  10.8 3.5 %collective-permute-start.4 = (bf16[512,1024]{1,0:T(8,128)(2,1)}, bf16[512,1024]{1,0:T(8,128)(2,1)S(1)}, u32[]{:S(2)}, u32[]{:S(2)}) collective-permute-start(bf16[512,1024]{1,0:T(8,128)(2,1)} %get-tuple-element.92), channel_id=1, source_target_pairs={{1,2},{3,4},{5,6},{7,8},{9,10},{11,12},{13,14},{15,16},{17,18},{19... | collective-permute-start | bytes 3145736 | tf_op jit(solution)/shard_map/ppermute | solution.py:565
  14.4 0.1 add_select_fusion.refs_1_
  14.5 0.1 add_select_fusion.1.bias_ref
  14.5 0.4 collective-permute-done.2.refs_3_
  14.9 1.7 %coarse_halos.1 = (bf16[4,384,256]{2,1,0:T(8,128)(2,1)S(1)}, bf16[768,256]{1,0:T(8,128)(2,1)S(1)}, bf16[768,256]{1,0:T(8,128)(2,1)S(1)}) custom-call(s32[2]{0:T(128)S(1)} %pad_add_fusion.refs_0_.place_ref, bf16[384,256]{1,0:T(8,128)(2,1)S(1)} %get-tuple-element.74.refs_0_, bf16[384,256]{1,0:T(8,128)(2,1)S(1)} %collective-permute-done.refs_1_, ...), custom_call_target="tpu_custom_call" | custom-call | flops 1048576 | bytes 2359296 | tf_op jit(solution)/shard_map/coarse_halos/pallas_call | solution.py:321
  16.6 3.2 %collective-permute-start.5 = (bf16[768,256]{1,0:T(8,128)(2,1)S(1)}, bf16[768,256]{1,0:T(8,128)(2,1)S(1)}, u32[]{:S(2)}, u32[]{:S(2)}) collective-permute-start(bf16[768,256]{1,0:T(8,128)(2,1)S(1)} %get-tuple-element.97), channel_id=1, source_target_pairs={{0,4},{4,8},{8,12},{12,16},{16,20},{20,24},{24,28},{1,5},{5,9},{9,... | collective-permute-start | bytes 1179656 | tf_op jit(solution)/shard_map/ppermute | solution.py:561
  19.8 2.1 %collective-permute-start.6 = (bf16[768,256]{1,0:T(8,128)(2,1)S(1)}, bf16[768,256]{1,0:T(8,128)(2,1)S(1)}, u32[]{:S(2)}, u32[]{:S(2)}) collective-permute-start(bf16[768,256]{1,0:T(8,128)(2,1)S(1)} %get-tuple-element.98), channel_id=1, source_target_pairs={{4,0},{8,4},{12,8},{16,12},{20,16},{24,20},{28,24},{5,1},{9,5},{13... | collective-permute-start | bytes 1179656 | tf_op jit(solution)/shard_map/ppermute | solution.py:561
  21.9 3.1 %collective-permute-start.7 = (bf16[256,1024]{1,0:T(8,128)(2,1)}, bf16[256,1024]{1,0:T(8,128)(2,1)S(1)}, u32[]{:S(2)}, u32[]{:S(2)}) collective-permute-start(bf16[256,1024]{1,0:T(8,128)(2,1)} %get-tuple-element.109), channel_id=1, source_target_pairs={{1,2},{3,4},{5,6},{7,8},{9,10},{11,12},{13,14},{15,16},{17,18},{19... | collective-permute-start | bytes 1572872 | tf_op jit(solution)/shard_map/ppermute | solution.py:565
  25.1 1.4 %collective-permute-start.3 = (bf16[768,1024]{1,0:T(8,128)(2,1)}, bf16[768,1024]{1,0:T(8,128)(2,1)S(1)}, u32[]{:S(2)}, u32[]{:S(2)}) collective-permute-start(bf16[768,1024]{1,0:T(8,128)(2,1)} %get-tuple-element.88), channel_id=1, source_target_pairs={{0,1},{2,3},{4,5},{6,7},{8,9},{10,11},{12,13},{14,15},{16,17},{18,... | collective-permute-start | bytes 4718600 | tf_op jit(solution)/shard_map/ppermute | solution.py:565
  26.4 4.8 %own_level.1 = (f32[4,512,256]{2,1,0:T(8,128)S(1)}, f32[4,512,256]{2,1,0:T(8,128)S(1)}, f32[4,512,256]{2,1,0:T(8,128)S(1)}) custom-call(bf16[512,1024]{1,0:T(8,128)(2,1)} %get-tuple-element.84.refs_0_.refs_2_, bf16[512,1024]{1,0:T(8,128)(2,1)} %refs_1_.4, bf16[512,1024]{1,0:T(8,128)(2,1)} %refs_2_.5), custom_call_target="tpu_custom_call" | custom-call | flops 68719476736 | bytes 1024 | tf_op jit(solution)/shard_map/own_level/pallas_call | solution.py:208
  31.2 5.0 %chip_level.1 = (f32[4,512,256]{2,1,0:T(8,128)S(1)}, f32[4,512,256]{2,1,0:T(8,128)S(1)}, f32[4,512,256]{2,1,0:T(8,128)S(1)}) custom-call(s32[2]{0:T(128)S(1)} %pad_add_fusion.refs_0_.place_ref, f32[2]{0:T(128)S(1)} %add_select_fusion.refs_1_, bf16[512,1024]{1,0:T(8,128)(2,1)} %get-tuple-element.84.refs_0_.refs_2_, ...), custom_call_target="tpu_custom_call" | custom-call | flops 1024 | bytes 1024 | tf_op jit(solution)/shard_map/chip_level/pallas_call | solution.py:208
  36.2 7.1 %collective-permute-done.4.refs_7_ = bf16[512,1024]{1,0:T(8,128)(2,1)S(1)} collective-permute-done((bf16[512,1024]{1,0:T(8,128)(2,1)}, bf16[512,1024]{1,0:T(8,128)(2,1)S(1)}, u32[]{:S(2)}, u32[]{:S(2)}) %collective-permute-start.4) | collective-permute-done | bytes 1048608 | tf_op jit(solution)/shard_map/ppermute | solution.py:565
  43.3 4.5 %near_level.1 = (f32[4,512,256]{2,1,0:T(8,128)S(1)}, f32[4,512,256]{2,1,0:T(8,128)S(1)}, f32[4,512,256]{2,1,0:T(8,128)S(1)}) custom-call(s32[2]{0:T(128)S(1)} %pad_add_fusion.refs_0_.place_ref, f32[2]{0:T(128)S(1)} %add_select_fusion.refs_1_, bf16[512,1024]{1,0:T(8,128)(2,1)} %get-tuple-element.84.refs_0_.refs_2_, ...), custom_call_target="tpu_custom_call" | custom-call | flops 1024 | bytes 1024 | tf_op jit(solution)/shard_map/near_level/pallas_call | solution.py:208
  47.8 4.0 %collective-permute-done.5.prev_ref = bf16[768,256]{1,0:T(8,128)(2,1)S(1)} collective-permute-done((bf16[768,256]{1,0:T(8,128)(2,1)S(1)}, bf16[768,256]{1,0:T(8,128)(2,1)S(1)}, u32[]{:S(2)}, u32[]{:S(2)}) %collective-permute-start.5) | collective-permute-done | bytes 393248 | tf_op jit(solution)/shard_map/ppermute | solution.py:561
  51.8 2.4 %coarse_levels.1 = (bf16[144,256]{1,0:T(8,128)(2,1)S(1)}, bf16[144,256]{1,0:T(8,128)(2,1)S(1)}, bf16[144,256]{1,0:T(8,128)(2,1)S(1)}, bf16[144,256]{1,0:T(8,128)(2,1)S(1)}) custom-call(s32[2]{0:T(128)S(1)} %pad_add_fusion.refs_0_.place_ref, f32[2]{0:T(128)S(1)} %add_select_fusion.1.bias_ref, bf16[4,384,256]{2,1,0:T(8,128)(2,1)S(1)} %get-tuple-element.96.got_ref, ...), custom_call_target="tpu_custom_call" | custom-call | flops 68719476736 | bytes 3145728 | tf_op jit(solution)/shard_map/coarse_levels/pallas_call | solution.py:429
  54.3 0.5 collective-permute-start.8
  54.8 1.7 %collective-permute-start.10 = (bf16[144,256]{1,0:T(8,128)(2,1)S(1)}, bf16[144,256]{1,0:T(8,128)(2,1)S(1)}, u32[]{:S(2)}, u32[]{:S(2)}) collective-permute-start(bf16[144,256]{1,0:T(8,128)(2,1)S(1)} %get-tuple-element.116), channel_id=1, source_target_pairs={{0,3},{1,2},{2,1},{3,0},{4,7},{5,6},{6,5},{7,4},{8,11},{9,10},{10,... | collective-permute-start | bytes 221192 | tf_op jit(solution)/shard_map/ppermute | solution.py:588
  56.5 3.9 %far_level.1 = (f32[4,512,256]{2,1,0:T(8,128)S(1)}, f32[4,512,256]{2,1,0:T(8,128)S(1)}, f32[4,512,256]{2,1,0:T(8,128)S(1)}) custom-call(s32[2]{0:T(128)S(1)} %pad_add_fusion.refs_0_.place_ref, f32[2]{0:T(128)S(1)} %add_select_fusion.refs_1_, bf16[256,1024]{1,0:T(8,128)(2,1)} %get-tuple-element.66.refs_3_.refs_2_, ...), custom_call_target="tpu_custom_call" | custom-call | flops 1024 | bytes 1024 | tf_op jit(solution)/shard_map/far_level/pallas_call | solution.py:208
  60.4 3.0 %finish.1 = bf16[512,1024]{1,0:T(8,128)(2,1)} custom-call(s32[2]{0:T(128)S(1)} %pad_add_fusion.refs_0_.place_ref, f32[4,512,256]{2,1,0:T(8,128)S(1)} %get-tuple-element.110.sum_ref, f32[4,512,256]{2,1,0:T(8,128)S(1)} %get-tuple-element.111.top_ref, f32[4,512,256]{2,1,0:T(8,128)S(1)} %get-tuple-element.112.total_ref, ...), custom_call_target="tpu_custom_call" | custom-call | flops 1024 | bytes 1024 | tf_op jit(solution)/shard_map/finish/pallas_call | solution.py:546
  (10 shorter events, 0.1 us)
Async XLA Ops:
  4.0 10.5 %collective-permute-start.1 = (bf16[384,256]{1,0:T(8,128)(2,1)S(1)}, bf16[384,256]{1,0:T(8,128)(2,1)S(1)}, u32[]{:S(2)}, u32[]{:S(2)}) collective-permute-start(bf16[384,256]{1,0:T(8,128)(2,1)S(1)} %get-tuple-element.71), channel_id=1, source_target_pairs={{0,2},{1,3},{2,0},{3,1},{4,6},{5,7},{6,4},{7,5},{8,10},{9,11},{10,... | collective-permute-start | bytes 589832 | tf_op jit(solution)/shard_map/ppermute | solution.py:588
  5.3 9.6 %collective-permute-start.2 = (bf16[384,256]{1,0:T(8,128)(2,1)S(1)}, bf16[384,256]{1,0:T(8,128)(2,1)S(1)}, u32[]{:S(2)}, u32[]{:S(2)}) collective-permute-start(bf16[384,256]{1,0:T(8,128)(2,1)S(1)} %get-tuple-element.72), channel_id=1, source_target_pairs={{0,3},{1,2},{2,1},{3,0},{4,7},{5,6},{6,5},{7,4},{8,11},{9,10},{10,... | collective-permute-start | bytes 589832 | tf_op jit(solution)/shard_map/ppermute | solution.py:588
  10.8 4.2 %collective-permute-start = (bf16[384,256]{1,0:T(8,128)(2,1)S(1)}, bf16[384,256]{1,0:T(8,128)(2,1)S(1)}, u32[]{:S(2)}, u32[]{:S(2)}) collective-permute-start(bf16[384,256]{1,0:T(8,128)(2,1)S(1)} %get-tuple-element.70), channel_id=1, source_target_pairs={{0,1},{1,0},{2,3},{3,2},{4,5},{5,4},{6,7},{7,6},{8,9},{9,8},{10,11... | collective-permute-start | bytes 589832 | tf_op jit(solution)/shard_map/ppermute | solution.py:588
  10.8 32.5 %collective-permute-start.4 = (bf16[512,1024]{1,0:T(8,128)(2,1)}, bf16[512,1024]{1,0:T(8,128)(2,1)S(1)}, u32[]{:S(2)}, u32[]{:S(2)}) collective-permute-start(bf16[512,1024]{1,0:T(8,128)(2,1)} %get-tuple-element.92), channel_id=1, source_target_pairs={{1,2},{3,4},{5,6},{7,8},{9,10},{11,12},{13,14},{15,16},{17,18},{19... | collective-permute-start | bytes 3145736 | tf_op jit(solution)/shard_map/ppermute | solution.py:565
  16.6 35.2 %collective-permute-start.5 = (bf16[768,256]{1,0:T(8,128)(2,1)S(1)}, bf16[768,256]{1,0:T(8,128)(2,1)S(1)}, u32[]{:S(2)}, u32[]{:S(2)}) collective-permute-start(bf16[768,256]{1,0:T(8,128)(2,1)S(1)} %get-tuple-element.97), channel_id=1, source_target_pairs={{0,4},{4,8},{8,12},{12,16},{16,20},{20,24},{24,28},{1,5},{5,9},{9,... | collective-permute-start | bytes 1179656 | tf_op jit(solution)/shard_map/ppermute | solution.py:561
  19.8 32.0 %collective-permute-start.6 = (bf16[768,256]{1,0:T(8,128)(2,1)S(1)}, bf16[768,256]{1,0:T(8,128)(2,1)S(1)}, u32[]{:S(2)}, u32[]{:S(2)}) collective-permute-start(bf16[768,256]{1,0:T(8,128)(2,1)S(1)} %get-tuple-element.98), channel_id=1, source_target_pairs={{4,0},{8,4},{12,8},{16,12},{20,16},{24,20},{28,24},{5,1},{9,5},{13... | collective-permute-start | bytes 1179656 | tf_op jit(solution)/shard_map/ppermute | solution.py:561
  21.9 34.5 %collective-permute-start.7 = (bf16[256,1024]{1,0:T(8,128)(2,1)}, bf16[256,1024]{1,0:T(8,128)(2,1)S(1)}, u32[]{:S(2)}, u32[]{:S(2)}) collective-permute-start(bf16[256,1024]{1,0:T(8,128)(2,1)} %get-tuple-element.109), channel_id=1, source_target_pairs={{1,2},{3,4},{5,6},{7,8},{9,10},{11,12},{13,14},{15,16},{17,18},{19... | collective-permute-start | bytes 1572872 | tf_op jit(solution)/shard_map/ppermute | solution.py:565
  25.1 6.1 %collective-permute-start.3 = (bf16[768,1024]{1,0:T(8,128)(2,1)}, bf16[768,1024]{1,0:T(8,128)(2,1)S(1)}, u32[]{:S(2)}, u32[]{:S(2)}) collective-permute-start(bf16[768,1024]{1,0:T(8,128)(2,1)} %get-tuple-element.88), channel_id=1, source_target_pairs={{0,1},{2,3},{4,5},{6,7},{8,9},{10,11},{12,13},{14,15},{16,17},{18,... | collective-permute-start | bytes 4718600 | tf_op jit(solution)/shard_map/ppermute | solution.py:565
  54.3 6.1 %collective-permute-start.8 = (bf16[144,256]{1,0:T(8,128)(2,1)S(1)}, bf16[144,256]{1,0:T(8,128)(2,1)S(1)}, u32[]{:S(2)}, u32[]{:S(2)}) collective-permute-start(bf16[144,256]{1,0:T(8,128)(2,1)S(1)} %get-tuple-element.114), channel_id=1, source_target_pairs={{0,1},{1,0},{2,3},{3,2},{4,5},{5,4},{6,7},{7,6},{8,9},{9,8},{10,11... | collective-permute-start | bytes 221192 | tf_op jit(solution)/shard_map/ppermute | solution.py:588
  54.7 5.6 %collective-permute-start.9 = (bf16[144,256]{1,0:T(8,128)(2,1)S(1)}, bf16[144,256]{1,0:T(8,128)(2,1)S(1)}, u32[]{:S(2)}, u32[]{:S(2)}) collective-permute-start(bf16[144,256]{1,0:T(8,128)(2,1)S(1)} %get-tuple-element.115), channel_id=1, source_target_pairs={{0,2},{1,3},{2,0},{3,1},{4,6},{5,7},{6,4},{7,5},{8,10},{9,11},{10,... | collective-permute-start | bytes 221192 | tf_op jit(solution)/shard_map/ppermute | solution.py:588
  54.8 5.6 %collective-permute-start.10 = (bf16[144,256]{1,0:T(8,128)(2,1)S(1)}, bf16[144,256]{1,0:T(8,128)(2,1)S(1)}, u32[]{:S(2)}, u32[]{:S(2)}) collective-permute-start(bf16[144,256]{1,0:T(8,128)(2,1)S(1)} %get-tuple-element.116), channel_id=1, source_target_pairs={{0,3},{1,2},{2,1},{3,0},{4,7},{5,6},{6,5},{7,4},{8,11},{9,10},{10,... | collective-permute-start | bytes 221192 | tf_op jit(solution)/shard_map/ppermute | solution.py:588
